TPU v7x, 32 devices: a whole 2x2x4 slice. The times are simulated.
32 devices in a mesh: rows: 8 (over z, x), blk: 4 (over y, core).
Axes of the slice: x: 2, y: 2, z: 4, core: 2. Of those that a mesh axis runs over, the one named last changes fastest.
Arguments:
- tokens: bfloat16 [64, 512, 768], P('rows', 'blk'), may hold values from -6 to 6
- lengths: int32 [64, 8], P('rows'), may hold values from 1 to 385, 512 in all within a row
- input_weight: bfloat16 [768, 2304], replicated, may hold values from -0.21875 to 0.21875
- query_bias: float32 [768], replicated, may hold values from -3 to 3
- value_bias: float32 [768], replicated, may hold values from -3 to 3
- output_weight: bfloat16 [768, 768], replicated, may hold values from -1.75 to 1.75
- output_bias: float32 [768], replicated, may hold values from -3 to 3
- first_gain: float32 [768], replicated, may hold values from 0.1 to 1.9
- first_shift: float32 [768], replicated, may hold values from -3 to 3
- up_weight: bfloat16 [768, 3072], replicated, may hold values from -0.21875 to 0.21875
- up_bias: float32 [3072], replicated, may hold values from -3 to 3
- down_weight: bfloat16 [3072, 768], replicated, may hold values from -0.109375 to 0.109375
- down_bias: float32 [768], replicated, may hold values from -3 to 3
- second_gain: float32 [768], replicated, may hold values from 0.1 to 1.9
- second_shift: float32 [768], replicated, may hold values from -3 to 3
- out_grad: bfloat16 [64, 512, 768], P('rows', 'blk'), may hold values from -6 to 6
- pool_grad: bfloat16 [64, 8, 768], P('rows'), may hold values from -96 to 96
Outputs:
- hidden_out: bfloat16 [64, 512, 768], P('rows', 'blk')
- pooled: float32 [64, 8, 768], P('rows')
- tokens_grad: float32 [64, 512, 768], P('rows', 'blk')
- input_weight_grad: float32 [768, 2304], replicated
- query_bias_grad: float32 [768], replicated
- value_bias_grad: float32 [768], replicated
- output_weight_grad: float32 [768, 768], replicated
- output_bias_grad: float32 [768], replicated
- first_gain_grad: float32 [768], replicated
- first_shift_grad: float32 [768], replicated
- up_weight_grad: float32 [768, 3072], replicated
- up_bias_grad: float32 [3072], replicated
- down_weight_grad: float32 [3072, 768], replicated
- down_bias_grad: float32 [768], replicated
- second_gain_grad: float32 [768], replicated
- second_shift_grad: float32 [768], replicated
Inputs may be any that keep to these rules, and one draw needn't show every extreme that they name: Each row's lengths sum to 512.
All inputs are finite; a program needn't handle non-finite values.
Results may differ from a plain program's by a relative error of at most 0.01.
Values may be sent and summed in bfloat16 or wider, within the bound.
No kernel may reach another device: no remote copies, remote signals or barrier semaphores. Data moves between devices by JAX's collectives and lax.ppermute only.
A program may use at most 256 MiB of HBM per device.

v0:
```python
import jax
import jax.numpy as jnp
from jax import lax
from jax.sharding import PartitionSpec as P

D = 768
H = 12
DH = 64
NSEG = 8


FINEST_PRECISION = lax.Precision.HIGHEST
NORM_EPS = 1e-12
MASKED = -1000000000.0


def layer_norm(hidden, gain, shift):
    center = hidden - jnp.mean(hidden, axis=-1, keepdims=True)
    spread = jnp.mean(center * center, axis=-1, keepdims=True)
    return center * lax.rsqrt(spread + NORM_EPS) * gain + shift


def segment_of(lengths, start, count):
    ends = jnp.cumsum(lengths, axis=-1)
    places = start + jnp.arange(count, dtype=jnp.int32)
    return jnp.sum((places[None, :, None] >= ends[:, None, :]).astype(jnp.int32), axis=-1)


def gelu_exact(value):
    return jax.nn.gelu(value, approximate=False)


def matmul(left, right):
    return jnp.dot(left, right, preferred_element_type=jnp.float32)


def left_product(left, right):
    return lax.dot_general(
        left, right, (((0,), (0,)), ((), ())), preferred_element_type=jnp.float32
    )


def right_matmul_output(left, right):
    return lax.dot_general(
        left, right, (((1,), (1,)), ((), ())), preferred_element_type=jnp.float32
    )


def on_device(
    tokens,
    lengths,
    input_weight,
    query_bias,
    value_bias,
    output_weight,
    output_bias,
    first_gain,
    first_shift,
    up_weight,
    up_bias,
    down_weight,
    down_bias,
    second_gain,
    second_shift,
    out_grad,
    pool_grad,
):
    batch, block, width = tokens.shape
    nblocks = lax.axis_size("blk")
    length = block * nblocks
    labels_local = segment_of(lengths, lax.axis_index("blk") * block, block)
    labels_whole = segment_of(lengths, 0, length)
    counts = lengths.astype(jnp.float32)
    segment_indicator = (labels_local[..., None] == jnp.arange(NSEG, dtype=jnp.int32)).astype(
        jnp.float32
    )
    total_rows = batch * block
    inputs = tokens.reshape(total_rows, width)
    bias = jnp.concatenate([query_bias, jnp.zeros_like(query_bias), value_bias])
    packed = (matmul(inputs, input_weight) + bias).astype(jnp.bfloat16)
    query_heads = packed[:, :D].reshape(batch, block, H, DH)
    key_block = packed[:, D : 2 * D].reshape(batch, block, D)
    value_block = packed[:, 2 * D :].reshape(batch, block, D)
    key_whole, value_whole = (
        lax.all_gather(key_block, "blk", axis=1, tiled=True),
        lax.all_gather(value_block, "blk", axis=1, tiled=True),
    )
    key_heads = key_whole.reshape(batch, length, H, DH)
    value_heads = value_whole.reshape(batch, length, H, DH)
    same = labels_local[:, None, :, None] == labels_whole[:, None, None, :]
    factor = DH ** (-0.5)
    scores = (
        jnp.einsum("bqhe,bkhe->bhqk", query_heads, key_heads, preferred_element_type=jnp.float32)
        * factor
    )
    scores = jnp.where(same, scores, MASKED)
    highest = jnp.max(scores, axis=-1, keepdims=True)
    probs = jnp.exp(scores - highest)
    probs = probs / jnp.sum(probs, axis=-1, keepdims=True)
    probs_low = probs.astype(jnp.bfloat16)
    mixed = jnp.einsum(
        "bhqk,bkhe->bqhe", probs_low, value_heads, preferred_element_type=jnp.float32
    )
    mixed = mixed.reshape(total_rows, width).astype(jnp.bfloat16)
    branch = matmul(mixed, output_weight) + output_bias
    first_in = inputs.astype(jnp.float32) + branch
    first = layer_norm(first_in, first_gain, first_shift)
    first_low = first.astype(jnp.bfloat16)
    inner = matmul(first_low, up_weight) + up_bias
    active_low = gelu_exact(inner).astype(jnp.bfloat16)
    second_in = first + matmul(active_low, down_weight) + down_bias
    layer_result = layer_norm(second_in, second_gain, second_shift)
    result_rows = layer_result.reshape(batch, block, width)
    partial_pool = jnp.einsum(
        "btc,btd->bcd", segment_indicator, result_rows, precision=FINEST_PRECISION
    )
    pooled = (
        lax.psum(partial_pool.astype(jnp.bfloat16), "blk").astype(jnp.float32) / counts[..., None]
    )
    pooling_fraction = pool_grad.astype(jnp.float32) / counts[..., None]
    grad_result = out_grad.astype(jnp.float32) + jnp.einsum(
        "btc,bcd->btd", segment_indicator, pooling_fraction, precision=FINEST_PRECISION
    )
    grad_result = grad_result.reshape(total_rows, width)
    unused, pull_second = jax.vjp(layer_norm, second_in, second_gain, second_shift)
    grad_second, grad_second_gain, grad_second_shift = pull_second(grad_result)
    grad_outer = grad_second.astype(jnp.bfloat16)
    grad_down_bias = jnp.sum(grad_outer.astype(jnp.float32), axis=0)
    grad_down = left_product(active_low, grad_outer)
    grad_active = right_matmul_output(grad_outer, down_weight)
    unused, pull_gelu = jax.vjp(gelu_exact, inner)
    grad_inner = pull_gelu(grad_active)[0].astype(jnp.bfloat16)
    grad_up_bias = jnp.sum(grad_inner.astype(jnp.float32), axis=0)
    grad_up = left_product(first_low, grad_inner)
    grad_first = grad_second + right_matmul_output(grad_inner, up_weight)
    unused, pull_first = jax.vjp(layer_norm, first_in, first_gain, first_shift)
    grad_first_in, grad_first_gain, grad_first_shift = pull_first(grad_first)
    grad_branch = grad_first_in.astype(jnp.bfloat16)
    grad_output_bias = jnp.sum(grad_branch.astype(jnp.float32), axis=0)
    grad_output = left_product(mixed, grad_branch)
    grad_mixed = (
        right_matmul_output(grad_branch, output_weight)
        .astype(jnp.bfloat16)
        .reshape(batch, block, H, DH)
    )
    grad_probs = jnp.einsum(
        "bqhe,bkhe->bhqk", grad_mixed, value_heads, preferred_element_type=jnp.float32
    )
    grad_value = jnp.einsum(
        "bhqk,bqhe->bkhe", probs_low, grad_mixed, preferred_element_type=jnp.float32
    )
    inner_sum = jnp.sum(grad_probs * probs, axis=-1, keepdims=True)
    grad_scores = jnp.where(same, probs * (grad_probs - inner_sum), 0.0).astype(jnp.bfloat16)
    grad_query = (
        jnp.einsum("bhqk,bkhe->bqhe", grad_scores, key_heads, preferred_element_type=jnp.float32)
        * factor
    )
    key_gradient = (
        jnp.einsum("bhqk,bqhe->bkhe", grad_scores, query_heads, preferred_element_type=jnp.float32)
        * factor
    )
    grad_key_block, grad_value_block = (
        lax.psum_scatter(
            key_gradient.reshape(batch, length, width).astype(jnp.bfloat16),
            "blk",
            scatter_dimension=1,
            tiled=True,
        ).astype(jnp.float32),
        lax.psum_scatter(
            grad_value.reshape(batch, length, width).astype(jnp.bfloat16),
            "blk",
            scatter_dimension=1,
            tiled=True,
        ).astype(jnp.float32),
    )
    grad_packed = jnp.concatenate(
        [
            grad_query.reshape(total_rows, width),
            grad_key_block.reshape(total_rows, width),
            grad_value_block.reshape(total_rows, width),
        ],
        axis=1,
    ).astype(jnp.bfloat16)
    packed_sum = jnp.sum(grad_packed.astype(jnp.float32), axis=0)
    grad_query_bias = packed_sum[:D]
    grad_value_bias = packed_sum[2 * D :]
    grad_input = left_product(inputs, grad_packed)
    grad_tokens = grad_first_in + right_matmul_output(grad_packed, input_weight)
    totals = lax.psum(
        (
            grad_input,
            grad_query_bias,
            grad_value_bias,
            grad_output,
            grad_output_bias,
            grad_first_gain,
            grad_first_shift,
            grad_up,
            grad_up_bias,
            grad_down,
            grad_down_bias,
            grad_second_gain,
            grad_second_shift,
        ),
        ("rows", "blk"),
    )
    return (
        result_rows.astype(jnp.bfloat16),
        pooled,
        grad_tokens.reshape(batch, block, width),
        totals[0],
        totals[1],
        totals[2],
        totals[3],
        totals[4],
        totals[5],
        totals[6],
        totals[7],
        totals[8],
        totals[9],
        totals[10],
        totals[11],
        totals[12],
    )


def solution(mesh):
    return jax.shard_map(
        on_device,
        mesh=mesh,
        in_specs=(
            P("rows", "blk", None),
            P("rows", None),
            P(),
            P(),
            P(),
            P(),
            P(),
            P(),
            P(),
            P(),
            P(),
            P(),
            P(),
            P(),
            P(),
            P("rows", "blk", None),
            P("rows", None, None),
        ),
        out_specs=(
            P("rows", "blk", None),
            P("rows", None, None),
            P("rows", "blk", None),
            P(),
            P(),
            P(),
            P(),
            P(),
            P(),
            P(),
            P(),
            P(),
            P(),
            P(),
            P(),
            P(),
        ),
        check_vma=False,
    )
```

profile of v0, /device:TPU:0, one launch (start us, length us, event | category | flops | bytes accessed | tf_op | source)
XLA Modules:
  0.0 983.3 jit_solution(9291832410073498376)
XLA Ops:
  31.7 35.0 %all-gather.5.cloned.1.call-done = bf16[8,512,768]{2,1,0:T(8,128)(2,1)} async-done(((bf16[8,128,768]{2,1,0:T(8,128)(2,1)}), bf16[8,512,768]{2,1,0:T(8,128)(2,1)}) %all-gather.5.cloned.1.call-update) | async-done | bytes 6291472 | tf_op jit(solution)/shard_map/all_gather | solution.py:85
  66.6 8.6 copy.57
  75.3 17.8 %fusion.83 = (f32[8,12,128]{2,1,0:T(8,128)}, f32[8,12,128,512]{3,2,1,0:T(8,128)}) fusion(pred[8,128,512]{2,1,0:T(8,128)(4,1)} %broadcast_compare_fusion, bf16[8,512,12,64]{1,3,2,0:T(8,128)(2,1)} %bitcast.91, bf16[8,128,12,64]{1,0,3,2:T(8,128)(2,1)} %bitcast.105), kind=kOutput, calls=%fused_computation.119 | convolution fusion | flops 830472704 | bytes 33603584 | tf_op jit(solution)/shard_map/sub | solution.py:98
  93.0 22.2 %all-gather.3.cloned.1.call-done = bf16[8,512,768]{2,1,0:T(8,128)(2,1)} async-done(((bf16[8,128,768]{2,1,0:T(8,128)(2,1)}), bf16[8,512,768]{2,1,0:T(8,128)(2,1)}) %all-gather.3.cloned.1.call-update) | async-done | bytes 6291472 | tf_op jit(solution)/shard_map/all_gather | solution.py:86
  115.2 8.6 copy.55
  123.8 12.6 %fusion.44 = bf16[8,128,12,64]{1,3,2,0:T(8,128)(2,1)S(1)} fusion(bf16[8,512,12,64]{1,3,2,0:T(8,128)(2,1)} %bitcast.85, f32[8,12,128,512]{3,2,1,0:T(8,128)} %get-tuple-element.99, f32[8,12,128]{2,1,0:T(8,128)} %get-tuple-element.98), kind=kOutput, calls=%fused_computation.74 | convolution fusion | flops 818675712 | bytes 33079296 | tf_op jit(solution)/shard_map/bhqk,bkhe->bqhe/dot_general | solution.py:101
  142.4 38.0 %multiply_convert_fusion.1 = (bf16[1024,3072]{1,0:T(8,128)(2,1)S(1)}, f32[1024,3072]{1,0:T(8,128)}, f32[1024,3072]{1,0:T(8,128)}) fusion(f32[3072]{0:T(1024)S(1)} %copy-done.31, bf16[768,3072]{1,0:T(8,128)(2,1)} %param.26, f32[1024,768]{1,0:T(8,128)S(1)} %get-tuple-element.101, f32[768]{0:T(1024)S(1)} %copy-done.19, f32[768]{0:T(1024)S(1)} %copy-done.15, ...), kind=kOutput, calls=%fused_computation.15 | convolution fusion | flops 5043388416 | bytes 39348224 | tf_op jit(solution)/shard_map/dot_general | solution.py:34
  196.1 18.7 %convert_reduce_fusion = (f32[3072]{0:T(1024)}, bf16[1024,3072]{1,0:T(8,128)(2,1)}) fusion(f32[1024,3072]{1,0:T(8,128)} %get-tuple-element.91, bf16[1024,768]{1,0:T(8,128)(2,1)} %get-tuple-element.83, bf16[3072,768]{1,0:T(8,128)(2,1)} %param.28, f32[1024,3072]{1,0:T(8,128)} %get-tuple-element.102, f32[3072]{0:T(1024)S(1)} %copy-done.31), kind=kOutput, calls=%fused_computation.10 | convolution fusion | flops 4885312512 | bytes 37773312 | tf_op jit(solution)/shard_map/dot_general | solution.py:44
  214.8 11.0 %multiply_reduce_fusion.1 = (f32[768]{0:T(1024)}, f32[1024]{0:T(1024)S(1)}, f32[768]{0:T(1024)}, f32[1024,768]{1,0:T(8,128)S(1)}) fusion(f32[1024,768]{1,0:T(8,128)S(1)} %get-tuple-element.101, f32[1024]{0:T(1024)S(1)} %fusion.68, f32[1024]{0:T(1024)S(1)} %broadcast_multiply_fusion.1, f32[768]{0:T(1024)S(1)} %copy-done.15, ...), kind=kOutput, calls=%fused_computation.50 | convolution fusion | flops 4839699456 | bytes 20472832 | tf_op jit(solution)/shard_map/dot_general | solution.py:44
  239.4 14.6 %fusion.53 = f32[8,12,128,512]{3,2,1,0:T(8,128)} fusion(bf16[8,512,12,64]{1,3,2,0:T(8,128)(2,1)} %bitcast.86, bf16[8,128,12,64]{1,0,3,2:T(8,128)(2,1)S(1)} %bitcast.89), kind=kOutput, calls=%fused_computation.79 | convolution fusion | flops 805306368 | bytes 33030144 | tf_op jit(solution)/shard_map/bqhe,bkhe->bhqk/dot_general | solution.py:146
  253.9 81.6 %multiply_convert_fusion = bf16[8,12,64,512]{3,2,1,0:T(8,128)(2,1)} fusion(f32[8,12,128,512]{3,2,1,0:T(8,128)} %fusion.53, pred[8,128,512]{2,1,0:T(8,128)(4,1)} %broadcast_compare_fusion, bf16[8,128,12,64]{1,0,3,2:T(8,128)(2,1)} %bitcast.106, f32[8,12,128,512]{3,2,1,0:T(8,128)} %get-tuple-element.99, f32[8,12,128]{2,1,0:T(8,128)} %get-tuple-element.98), kind=kOutput, calls=%fused_computation.11 | convolution fusion | flops 855650816 | bytes 58769408 | tf_op jit(solution)/shard_map/bhqk,bqhe->bkhe/dot_general | solution.py:159
  335.5 8.7 copy.64
  344.3 15.3 %fusion.27 = bf16[8,12,64,512]{3,2,1,0:T(8,128)(2,1)} fusion(bf16[8,128,12,64]{1,0,3,2:T(8,128)(2,1)} %bitcast.90, f32[8,12,128,512]{3,2,1,0:T(8,128)} %get-tuple-element.99, f32[8,12,128]{2,1,0:T(8,128)} %get-tuple-element.98), kind=kOutput, calls=%fused_computation.45 | convolution fusion | flops 821035008 | bytes 33079296 | tf_op jit(solution)/shard_map/bhqk,bqhe->bkhe/dot_general | solution.py:149
  359.6 8.7 copy.66
  368.4 80.6 %fusion.47 = bf16[8,128,12,64]{1,3,2,0:T(8,128)(2,1)} fusion(bf16[8,512,12,64]{1,3,2,0:T(8,128)(2,1)} %bitcast.92, f32[8,12,128,512]{3,2,1,0:T(8,128)} %fusion.53, pred[8,128,512]{2,1,0:T(8,128)(4,1)} %broadcast_compare_fusion, f32[8,12,128,512]{3,2,1,0:T(8,128)} %get-tuple-element.99, f32[8,12,128]{2,1,0:T(8,128)} %get-tuple-element.98), kind=kOutput, calls=%fused_computation.75 | convolution fusion | flops 850932224 | bytes 58769408 | tf_op jit(solution)/shard_map/bhqk,bkhe->bqhe/dot_general | solution.py:155
  460.2 10.9 %fusion.74 = f32[768,3072]{1,0:T(8,128)} fusion(bf16[1024,3072]{1,0:T(8,128)(2,1)} %get-tuple-element.107, f32[1024,768]{1,0:T(8,128)S(1)} %copy-done.2, f32[768]{0:T(1024)S(1)} %copy-done.20, f32[768]{0:T(1024)S(1)} %copy-done.16, f32[1024]{0:T(1024)S(1)} %copy-done.14, f32[1024]{0:T(1024)S(1)} %copy-done.12), kind=kOutput, calls=%fused_computation.113 | convolution fusion | flops 4835770368 | bytes 18888704 | tf_op jit(solution)/shard_map/dot_general | solution.py:38
  471.0 8.0 fusion.91
  484.4 9.6 convolution_bitcast_fusion
  497.3 13.2 %all-reduce.5.cloned.1.call-done = bf16[8,8,768]{2,1,0:T(8,128)(2,1)} async-done(((bf16[8,8,768]{2,1,0:T(8,128)(2,1)}), bf16[8,8,768]{2,1,0:T(8,128)(2,1)}) %all-reduce.5.cloned.1.call-update) | async-done | bytes 98320 | tf_op jit(solution)/shard_map/psum | solution.py:118
  515.5 42.9 %all-reduce = (f32[768]{0:T(1024)}, f32[768]{0:T(1024)}, f32[768]{0:T(1024)}, f32[768]{0:T(1024)}, f32[768]{0:T(1024)}, /*index=5*/f32[3072]{0:T(1024)}, f32[768]{0:T(1024)}, f32[768]{0:T(1024)}, f32[768]{0:T(1024)}) all-reduce(f32[768]{0:T(1024)} %get-tuple-element.97, ...), channel_id=1, replica_groups=mesh['rows'=8,'blk'=4] {'rows','blk'}, use_global_device_ids=true, to_apply=%region_19.20 | all-reduce | flops 9216 | bytes 73728 | tf_op jit(solution)/shard_map/psum | solution.py:189
  558.4 9.2 add_add_fusion.4
  567.6 384.8 %all-reduce.7.cloned.1.call-done = (f32[768,2304]{0,1:T(8,128)}, f32[768,768]{1,0:T(8,128)}, f32[768,3072]{1,0:T(8,128)}, f32[3072,768]{1,0:T(8,128)}) async-done(((f32[768,2304]{0,1:T(8,128)}, f32[768,768]{1,0:T(8,128)}, f32[768,3072]{1,0:T(8,128)}, f32[3072,768]{1,0:T(8,128)}), (f32[768,2304]{0,1:T(8,128)}, f32[768,768]{1,0:T(8,128)}, f32[768,3072]{1,0:T(8,128)}, ...) | async-done | bytes 28311568 | tf_op jit(solution)/shard_map/psum | solution.py:189
  952.4 8.0 copy.69
  963.7 8.8 copy.110
  (147 shorter events, 91.2 us)
Async XLA Ops:
  7.2 59.4 %all-gather.5.cloned.1.call-start = ((), (), s32[]{:S(2)}) async-start(), calls=%async_computation.3 | async-start | bytes 7864320 | tf_op jit(solution)/shard_map/all_gather | solution.py:85
  17.4 97.8 %all-gather.3.cloned.1.call-start = ((), (), s32[]{:S(2)}) async-start(), calls=%async_computation.2 | async-start | bytes 7864320 | tf_op jit(solution)/shard_map/all_gather | solution.py:86
  18.2 461.0 %reduce-scatter.3.cloned.1.call-start = ((), (), s32[]{:S(2)}) async-start(), calls=%async_computation.5 | async-start | bytes 7864320 | tf_op jit(solution)/shard_map/reduce_scatter | solution.py:163
  18.7 12.9 %copy-start.21 = (f32[8,8]{1,0:T(8,128)}, f32[8,8]{1,0:T(8,128)S(1)}, u32[]{:S(2)}) copy-start(f32[8,8]{1,0:T(8,128)S(1)} %convert_element_type.110) | copy-start | bytes 772
  123.8 13.8 %copy-start.32 = (f32[768]{0:T(1024)S(1)}, f32[768]{0:T(1024)}, u32[]{:S(2)}) copy-start(f32[768]{0:T(1024)} %param.23) | copy-start | bytes 9220
  137.7 42.7 %slice-start.3 = ((s8[4718592]{0:T(1024)(128)(4,1)}), s8[4194304]{0:T(1024)(128)(4,1)S(1)}, s32[]{:S(2)}) async-start(s8[4718592]{0:T(1024)(128)(4,1)} %bitcast.109), calls=%async_computation.11 | async-start | bytes 8388608
  141.8 84.1 %copy-start.1 = (f32[1024,768]{1,0:T(8,128)}, f32[1024,768]{1,0:T(8,128)S(1)}, u32[]{:S(2)}) copy-start(f32[1024,768]{1,0:T(8,128)S(1)} %get-tuple-element.101) | copy-start | bytes 9437188
  141.8 84.1 %copy-start.11 = (f32[1024]{0:T(1024)}, f32[1024]{0:T(1024)S(1)}, u32[]{:S(2)}) copy-start(f32[1024]{0:T(1024)S(1)} %broadcast_multiply_fusion.1) | copy-start | bytes 12292
  142.3 83.5 %copy-start.13 = (f32[1024]{0:T(1024)}, f32[1024]{0:T(1024)S(1)}, u32[]{:S(2)}) copy-start(f32[1024]{0:T(1024)S(1)} %fusion.68) | copy-start | bytes 12292
  142.4 38.1 %slice-start.4 = ((s8[4718592]{0:T(1024)(128)(4,1)}), s8[524288]{0:T(1024)(128)(4,1)S(1)}, s32[]{:S(2)}) async-start(s8[4718592]{0:T(1024)(128)(4,1)} %bitcast.109), calls=%async_computation.12 | async-start | bytes 1048576
  142.4 38.1 %copy-start.33 = (f32[768]{0:T(1024)S(1)}, f32[768]{0:T(1024)}, u32[]{:S(2)}) copy-start(f32[768]{0:T(1024)} %param.29) | copy-start | bytes 9220
  344.3 137.5 %reduce-scatter.5.cloned.1.call-start = ((), (), s32[]{:S(2)}) async-start(), calls=%async_computation.6 | async-start | bytes 7864320 | tf_op jit(solution)/shard_map/reduce_scatter | solution.py:169
  368.4 142.1 %all-reduce.5.cloned.1.call-start = ((), (), s32[]{:S(2)}) async-start(), calls=%async_computation.4 | async-start | bytes 196608 | tf_op jit(solution)/shard_map/psum | solution.py:118
  455.3 15.8 %slice-start.5 = ((s8[6291456]{0:T(1024)(128)(4,1)}), s8[4194304]{0:T(1024)(128)(4,1)S(1)}, s32[]{:S(2)}) async-start(s8[6291456]{0:T(1024)(128)(4,1)} %bitcast.115), calls=%async_computation.13 | async-start | bytes 8388608
  460.1 10.9 %copy-start.9 = (bf16[1024,768]{1,0:T(8,128)(2,1)S(1)}, bf16[1024,768]{1,0:T(8,128)(2,1)}, u32[]{:S(2)}) copy-start(bf16[1024,768]{1,0:T(8,128)(2,1)} %get-tuple-element.83) | copy-start | bytes 4718596
  460.2 10.9 %slice-start.6 = ((s8[6291456]{0:T(1024)(128)(4,1)}), s8[2097152]{0:T(1024)(128)(4,1)S(1)}, s32[]{:S(2)}) async-start(s8[6291456]{0:T(1024)(128)(4,1)} %bitcast.115), calls=%async_computation.14 | async-start | bytes 4194304
  479.0 473.3 %all-reduce.7.cloned.1.call-start = ((), (), s32[]{:S(2)}) async-start(), calls=%async_computation.7 | async-start | bytes 56623104 | tf_op jit(solution)/shard_map/psum | solution.py:189
  494.0 16.5 %copy-start.22 = (f32[8,8]{1,0:T(8,128)S(1)}, f32[8,8]{1,0:T(8,128)}, u32[]{:S(2)}) copy-start(f32[8,8]{1,0:T(8,128)} %copy-done.21) | copy-start | bytes 772
  494.0 21.4 %copy-start.25 = (f32[768]{0:T(1024)S(1)}, f32[768]{0:T(1024)}, u32[]{:S(2)}) copy-start(f32[768]{0:T(1024)} %get-tuple-element.82) | copy-start | bytes 9220
  494.0 21.4 %copy-start.26 = (f32[768]{0:T(1024)S(1)}, f32[768]{0:T(1024)}, u32[]{:S(2)}) copy-start(f32[768]{0:T(1024)} %get-tuple-element.84) | copy-start | bytes 9220
  494.1 64.3 %copy-start.24 = (f32[1024]{0:T(1024)S(1)}, f32[1024]{0:T(1024)}, u32[]{:S(2)}) copy-start(f32[1024]{0:T(1024)} %copy-done.23) | copy-start | bytes 12292
  960.3 12.1 %slice-start = ((s8[9437184]{0:T(1024)(128)(4,1)}), s8[4194304]{0:T(1024)(128)(4,1)S(1)}, s32[]{:S(2)}) async-start(s8[9437184]{0:T(1024)(128)(4,1)} %bitcast.87), calls=%async_computation.8 | async-start | bytes 8388608
  963.7 8.8 slice-start.1
  963.7 8.8 slice-start.2
  (24 other events, 87.5 us)
Sparse Core Ops, SparseCore 0:
  17.5 49.0 all-gather.4
  68.8 46.3 all-gather.2
  344.4 58.4 reduce-scatter.2
  405.4 58.5 reduce-scatter.4
  479.2 31.2 all-reduce.4
  519.1 433.2 all-reduce.6
where the time goes:
time: 987 us; the launch traced here: 983 us
  waiting for transfers between devices  456 us (46%)
  matrix products  358 us (36%)
  local copies, waits for them, and re-layouts  90.6 us (9%)
  blocking collectives  42.9 us (4%)
  other arithmetic  20.1 us (2%)
  between operations  15 us (2%)
    psum x1, waiting for transfers between devices, on_device(): lax.psum((grad_input, grad_query_bias, grad_value_bias, grad_output, grad...  385 us
    dot_general x1, matrix products, on_device(): jnp.einsum('bhqk,bqhe->bkhe', grad_scores, query_heads, preferred_element...  81.6 us
    dot_general x1, matrix products, on_device(): jnp.einsum('bhqk,bkhe->bqhe', grad_scores, key_heads, preferred_element_t...  80.6 us
    dot_general x4, matrix products, matmul(): return jnp.dot(left, right, preferred_element_type=jnp.float32)  53.3 us
    psum x1, blocking collectives, on_device(): lax.psum((grad_input, grad_query_bias, grad_value_bias, grad_output, grad...  42.9 us
    dot_general x4, matrix products, right_matmul_output(): lax.dot_general(left, right, (((1,), (1,)), ((), ())), preferred_element_...  41.4 us
    unnamed x91, local copies, waits for them, and re-layouts  38.6 us
    all_gather x1, waiting for transfers between devices, on_device(): lax.all_gather(key_block, 'blk', axis=1, tiled=True)  35 us
  transfers between devices with their start and end apart: 6, of which 4 were waited for; matrix products, arithmetic and copies ran while one was open for 21% of the time, Pallas kernels for 0%

commit v1 on v0

v1 whole, which is shorter than its diff:
```python
import functools
import jax
import jax.numpy as jnp
from jax import lax
from jax.experimental import pallas as pl
from jax.experimental.pallas import tpu as pltpu
from jax.sharding import PartitionSpec as P

D = 768
H = 12
DH = 64
FF = 3072
NSEG = 8
PAIR = 2 * DH
NORM_EPS = 1e-12
BIG = 1e9
BF = jnp.bfloat16
F32 = jnp.float32
CHUNK = 512
VMEM_LIMIT = 60 * 1024 * 1024


def nn(a, b):
    return lax.dot_general(a, b, (((1,), (0,)), ((), ())), preferred_element_type=F32)


def nt(a, b):
    return lax.dot_general(a, b, (((1,), (1,)), ((), ())), preferred_element_type=F32)


def tn(a, b):
    return lax.dot_general(a, b, (((0,), (0,)), ((), ())), preferred_element_type=F32)


def col_sum(a):
    return jnp.sum(a, axis=0, keepdims=True)


def norm_parts(hidden):
    center = hidden - jnp.mean(hidden, axis=-1, keepdims=True)
    spread = jnp.mean(center * center, axis=-1, keepdims=True)
    inverse = lax.rsqrt(spread + NORM_EPS)
    return center * inverse, inverse


def norm_back(grad, gain, unit, inverse):
    scaled = grad * gain
    along = jnp.mean(scaled * unit, axis=-1, keepdims=True)
    return inverse * (scaled - jnp.mean(scaled, axis=-1, keepdims=True) - unit * along)


def segments(lengths_ref, row, shape, nblk, me):
    local = lax.broadcasted_iota(jnp.int32, shape, 0)
    block = shape[0] // nblk
    places = ((local // block) ^ me) * block + local % block
    end = jnp.int32(0)
    labels = jnp.zeros(shape, jnp.int32)
    for c in range(NSEG):
        end = end + lengths_ref[row, c]
        labels = labels + (places >= end).astype(jnp.int32)
    return labels


def on_blk():
    return lax.axis_index("blk")


def head_masks(length):
    lane = lax.broadcasted_iota(jnp.int32, (length, PAIR), 1)
    return lane < DH, lane >= DH


def attention_kernel(
    lengths_ref, tokens_ref, w_in_ref, bias_ref, w_out_ref, out_bias_ref,
    packed_ref, mixed_ref, first_in_ref, nblk, where, qblock=512,
):
    length = tokens_ref.shape[1]
    row = pl.program_id(0)
    x = tokens_ref[0]
    for c in range(3):
        cols = pl.ds(c * D, D)
        packed_ref[0, :, cols] = (nn(x, w_in_ref[:, cols]) + bias_ref[:, cols]).astype(BF)
    labels = segments(lengths_ref, row, (length, PAIR), nblk, where())
    lane = lax.broadcasted_iota(jnp.int32, (length, PAIR), 1)
    hit = labels == lane
    here = jnp.where(hit, 1.0, 0.0).astype(BF)
    away = jnp.where(hit, 0.0, -BIG).astype(BF)
    masks = head_masks(qblock)
    for j in range(H // 2):
        k = packed_ref[0, :, pl.ds(D + j * PAIR, PAIR)]
        v = packed_ref[0, :, pl.ds(2 * D + j * PAIR, PAIR)]
        k_aug = jnp.concatenate([k, away], axis=1)
        for t in range(length // qblock):
            rows = pl.ds(t * qblock, qblock)
            q = packed_ref[0, rows, pl.ds(j * PAIR, PAIR)] * jnp.asarray(DH**-0.5, BF)
            outs = []
            for h in range(2):
                qh = jnp.where(masks[h], q, jnp.zeros_like(q))
                s = nt(jnp.concatenate([qh, here[t * qblock : (t + 1) * qblock]], axis=1), k_aug)
                e = jnp.exp(s - jnp.max(s, axis=1, keepdims=True))
                total = jnp.sum(e, axis=1, keepdims=True)
                outs.append(nn(e.astype(BF), v) / total)
            mixed_ref[0, rows, pl.ds(j * PAIR, PAIR)] = jnp.where(masks[0], outs[0], outs[1]).astype(BF)
    branch = nn(mixed_ref[0], w_out_ref[...]) + out_bias_ref[...]
    first_in_ref[0] = x.astype(F32) + branch


def whole(shape):
    return pl.BlockSpec(shape, lambda *_: (0,) * len(shape), pipeline_mode=pl.Buffered(1))


def per_row(*shape):
    return pl.BlockSpec((1,) + shape, lambda r: (r,) + (0,) * len(shape))


SMEM = pl.BlockSpec(memory_space=pltpu.SMEM)


def attention_forward(lengths, tokens, w_in, bias, w_out, out_bias, nblk, where=on_blk, qblock=512):
    rows, length, _ = tokens.shape
    return pl.pallas_call(
        functools.partial(attention_kernel, nblk=nblk, where=where, qblock=qblock),
        grid=(rows,),
        in_specs=[SMEM, per_row(length, D), whole((D, 3 * D)), whole((1, 3 * D)), whole((D, D)), whole((1, D))],
        out_specs=[per_row(length, 3 * D), per_row(length, D), per_row(length, D)],
        out_shape=[
            jax.ShapeDtypeStruct((rows, length, 3 * D), BF),
            jax.ShapeDtypeStruct((rows, length, D), BF),
            jax.ShapeDtypeStruct((rows, length, D), F32),
        ],
        compiler_params=pltpu.CompilerParams(vmem_limit_bytes=VMEM_LIMIT),
        name="attention_forward",
    )(lengths, tokens, w_in, bias, w_out, out_bias)


def gelu_both(x):
    cdf = 0.5 + 0.5 * lax.erf(x * (0.5**0.5))
    density = jnp.exp(x * x * -0.5) * 0.3989422804014327
    return x * cdf, cdf + x * density


def feed_forward_kernel(
    lengths_ref, first_in_ref, w_up_ref, up_bias_ref, w_down_ref, down_bias_ref,
    g1_ref, b1_ref, g2_ref, b2_ref, out_grad_ref, pool_grad_ref,
    hidden_ref, pooled_ref, slope_ref, grad_second_ref, down_grad_ref, vec_ref,
    active_ref, outer_ref, nblk, where,
):
    r = pl.program_id(0)
    nrows = pl.num_programs(0)
    length = first_in_ref.shape[1]
    row = r
    unit, _ = norm_parts(first_in_ref[0])
    first = unit * g1_ref[...] + b1_ref[...]
    low = first.astype(BF)
    here_rows = pl.ds(pl.multiple_of(r * length, length), length)
    acc = first + down_bias_ref[...]
    for c in range(FF // CHUNK):
        cols = pl.ds(c * CHUNK, CHUNK)
        inner = nn(low, w_up_ref[:, cols]) + up_bias_ref[:, cols]
        act, slope = gelu_both(inner)
        act = act.astype(BF)
        active_ref[here_rows, cols] = act
        slope_ref[0, :, cols] = slope.astype(BF)
        acc = acc + nn(act, w_down_ref[cols, :])
    unit, inverse = norm_parts(acc)
    result = unit * g2_ref[...] + b2_ref[...]
    hidden_ref[0] = result.astype(BF)
    lane = lax.broadcasted_iota(jnp.int32, (length, PAIR), 1)
    hit = segments(lengths_ref, row, (length, PAIR), nblk, where()) == lane
    here = jnp.where(hit, 1.0, 0.0).astype(BF)
    high = result.astype(BF)
    rest = (result - high.astype(F32)).astype(BF)
    sums = (tn(here, high) + tn(here, rest))[:NSEG]
    sub = lax.broadcasted_iota(jnp.int32, (NSEG, 1), 0)
    count = jnp.zeros((NSEG, 1), F32)
    for c in range(NSEG):
        count = jnp.where(sub == c, lengths_ref[row, c].astype(F32), count)
    pooled_ref[0] = sums / count
    share = pool_grad_ref[0].astype(F32) / count
    share_high = share.astype(BF)
    share_rest = (share - share_high.astype(F32)).astype(BF)
    pad = jnp.zeros((PAIR - NSEG, D), BF)
    spread = nn(here, jnp.concatenate([share_high, pad], axis=0)) + nn(here, jnp.concatenate([share_rest, pad], axis=0))
    grad = out_grad_ref[0].astype(F32) + spread
    grad_second = norm_back(grad, g2_ref[...], unit, inverse)
    grad_second_ref[0] = grad_second
    outer = grad_second.astype(BF)
    outer_ref[here_rows, :] = outer
    sums = jnp.concatenate(
        [col_sum(grad * unit), col_sum(grad), col_sum(outer.astype(F32)), jnp.zeros((5, D), F32)], axis=0
    )

    @pl.when(r == 0)
    def _():
        vec_ref[...] = sums

    @pl.when(r != 0)
    def _():
        vec_ref[...] += sums

    @pl.when(r == nrows - 1)
    def _():
        for c in range(FF // CHUNK):
            cols = pl.ds(c * CHUNK, CHUNK)
            down_grad_ref[cols, :] = tn(active_ref[:, cols], outer_ref[...]).astype(BF)


def feed_forward(lengths, first_in, w_up, up_bias, w_down, down_bias, g1, b1, g2, b2, out_grad, pool_grad, nblk, where=on_blk):
    rows, length, _ = first_in.shape
    vec = whole((1, D))
    return pl.pallas_call(
        functools.partial(feed_forward_kernel, nblk=nblk, where=where),
        grid=(rows,),
        in_specs=[SMEM, per_row(length, D), whole((D, FF)), whole((1, FF)), whole((FF, D)), vec, vec, vec, vec, vec,
                  per_row(length, D), per_row(NSEG, D)],
        out_specs=[per_row(length, D), per_row(NSEG, D), per_row(length, FF), per_row(length, D), whole((FF, D)), whole((8, D))],
        out_shape=[
            jax.ShapeDtypeStruct((rows, length, D), BF),
            jax.ShapeDtypeStruct((rows, NSEG, D), F32),
            jax.ShapeDtypeStruct((rows, length, FF), BF),
            jax.ShapeDtypeStruct((rows, length, D), F32),
            jax.ShapeDtypeStruct((FF, D), BF),
            jax.ShapeDtypeStruct((8, D), F32),
        ],
        scratch_shapes=[pltpu.VMEM((rows * length, FF), BF), pltpu.VMEM((rows * length, D), BF)],
        compiler_params=pltpu.CompilerParams(vmem_limit_bytes=VMEM_LIMIT),
        name="feed_forward",
    )(lengths, first_in, w_up, up_bias, w_down, down_bias, g1, b1, g2, b2, out_grad, pool_grad)


def feed_back_kernel(
    first_in_ref, slope_ref, grad_second_ref, mixed_ref, w_up_ref, w_down_ref, w_out_ref, g1_ref, b1_ref,
    grad_first_in_ref, grad_mixed_ref, up_grad_ref, output_grad_ref, vec_ref, up_bias_ref,
    low_ref, inner_ref, branch_ref, mix_ref,
):
    r = pl.program_id(0)
    nrows = pl.num_programs(0)
    length = first_in_ref.shape[1]
    here_rows = pl.ds(pl.multiple_of(r * length, length), length)
    grad_second = grad_second_ref[0]
    outer = grad_second.astype(BF)
    acc = grad_second

    @pl.when(r == 0)
    def _():
        vec_ref[...] = jnp.zeros_like(vec_ref)
        up_bias_ref[...] = jnp.zeros_like(up_bias_ref)

    for c in range(FF // CHUNK):
        cols = pl.ds(c * CHUNK, CHUNK)
        grad_active = nt(outer, w_down_ref[cols, :])
        inner = (grad_active * slope_ref[0, :, cols].astype(F32)).astype(BF)
        inner_ref[here_rows, cols] = inner
        up_bias_ref[:, cols] += col_sum(inner.astype(F32))
        acc = acc + nt(inner, w_up_ref[:, cols])
    unit, inverse = norm_parts(first_in_ref[0])
    low_ref[here_rows, :] = (unit * g1_ref[...] + b1_ref[...]).astype(BF)
    grad_first_in = norm_back(acc, g1_ref[...], unit, inverse)
    grad_first_in_ref[0] = grad_first_in
    branch = grad_first_in.astype(BF)
    branch_ref[here_rows, :] = branch
    mix_ref[here_rows, :] = mixed_ref[0]
    vec_ref[...] += jnp.concatenate(
        [col_sum(acc * unit), col_sum(acc), col_sum(branch.astype(F32)), jnp.zeros((5, D), F32)], axis=0
    )
    grad_mixed_ref[0] = nt(branch, w_out_ref[...]).astype(BF)

    @pl.when(r == nrows - 1)
    def _():
        for c in range(FF // CHUNK):
            cols = pl.ds(c * CHUNK, CHUNK)
            up_grad_ref[:, cols] = tn(low_ref[...], inner_ref[:, cols]).astype(BF)
        output_grad_ref[...] = tn(mix_ref[...], branch_ref[...]).astype(BF)


def feed_back(first_in, slope, grad_second, mixed, w_up, w_down, w_out, g1, b1):
    rows, length, _ = first_in.shape
    return pl.pallas_call(
        feed_back_kernel,
        grid=(rows,),
        in_specs=[per_row(length, D), per_row(length, FF), per_row(length, D), per_row(length, D),
                  whole((D, FF)), whole((FF, D)), whole((D, D)), whole((1, D)), whole((1, D))],
        out_specs=[per_row(length, D), per_row(length, D), whole((D, FF)), whole((D, D)), whole((8, D)), whole((1, FF))],
        out_shape=[
            jax.ShapeDtypeStruct((rows, length, D), F32),
            jax.ShapeDtypeStruct((rows, length, D), BF),
            jax.ShapeDtypeStruct((D, FF), BF),
            jax.ShapeDtypeStruct((D, D), BF),
            jax.ShapeDtypeStruct((8, D), F32),
            jax.ShapeDtypeStruct((1, FF), F32),
        ],
        scratch_shapes=[pltpu.VMEM((rows * length, D), BF), pltpu.VMEM((rows * length, FF), BF),
                        pltpu.VMEM((rows * length, D), BF), pltpu.VMEM((rows * length, D), BF)],
        compiler_params=pltpu.CompilerParams(vmem_limit_bytes=VMEM_LIMIT),
        name="feed_back",
    )(first_in, slope, grad_second, mixed, w_up, w_down, w_out, g1, b1)


def attention_back_kernel(
    lengths_ref, tokens_ref, packed_ref, grad_mixed_ref, grad_first_in_ref, w_in_ref,
    tokens_grad_ref, input_grad_ref, vec_ref, x_ref, grad_packed_ref, nblk, where,
):
    r = pl.program_id(0)
    nrows = pl.num_programs(0)
    length = tokens_ref.shape[1]
    row = r
    here_rows = pl.ds(pl.multiple_of(r * length, length), length)
    x_ref[here_rows, :] = tokens_ref[0]
    labels = segments(lengths_ref, row, (length, PAIR), nblk, where())
    lane = lax.broadcasted_iota(jnp.int32, (length, PAIR), 1)
    hit = labels == lane
    here = jnp.where(hit, 1.0, 0.0).astype(BF)
    away = jnp.where(hit, 0.0, -BIG).astype(BF)
    masks = head_masks(length)
    scale = DH**-0.5
    for j in range(H // 2):
        q = packed_ref[0, :, pl.ds(j * PAIR, PAIR)] * jnp.asarray(scale, BF)
        k = packed_ref[0, :, pl.ds(D + j * PAIR, PAIR)]
        v = packed_ref[0, :, pl.ds(2 * D + j * PAIR, PAIR)]
        gm = grad_mixed_ref[0, :, pl.ds(j * PAIR, PAIR)]
        k_aug = jnp.concatenate([k, away], axis=1)
        gq = gk = gv = None
        for h in range(2):
            zero = jnp.zeros_like(q)
            qh = jnp.where(masks[h], q, zero)
            kh = jnp.where(masks[h], k, zero)
            gmh = jnp.where(masks[h], gm, zero)
            s = nt(k_aug, jnp.concatenate([qh, here], axis=1))
            e = jnp.exp(s - jnp.max(s, axis=0, keepdims=True))
            p = e * (1.0 / jnp.sum(e, axis=0, keepdims=True))
            gp = nt(v, gmh)
            delta = jnp.sum(gp * p, axis=0, keepdims=True)
            gs = (p * (gp - delta)).astype(BF)
            gvh = nn(p.astype(BF), gmh)
            gkh = nn(gs, qh)
            gqh = tn(gs, kh)
            gq, gk, gv = (gqh, gkh, gvh) if h == 0 else (gq + gqh, gk + gkh, gv + gvh)
        grad_packed_ref[here_rows, pl.ds(j * PAIR, PAIR)] = (gq * scale).astype(BF)
        grad_packed_ref[here_rows, pl.ds(D + j * PAIR, PAIR)] = gk.astype(BF)
        grad_packed_ref[here_rows, pl.ds(2 * D + j * PAIR, PAIR)] = gv.astype(BF)
    gpk = grad_packed_ref[here_rows, :]
    tokens_grad_ref[0] = (grad_first_in_ref[0] + nt(gpk, w_in_ref[...])).astype(tokens_grad_ref.dtype)
    sums = jnp.concatenate(
        [col_sum(gpk[:, :D].astype(F32)), col_sum(gpk[:, 2 * D :].astype(F32)), jnp.zeros((6, D), F32)], axis=0
    )

    @pl.when(r == 0)
    def _():
        vec_ref[...] = sums

    @pl.when(r != 0)
    def _():
        vec_ref[...] += sums

    @pl.when(r == nrows - 1)
    def _():
        for c in range(3):
            cols = pl.ds(c * D, D)
            input_grad_ref[:, cols] = tn(x_ref[...], grad_packed_ref[:, cols]).astype(BF)


def attention_back(lengths, tokens, packed, grad_mixed, grad_first_in, w_in, nblk, where=on_blk):
    rows, length, _ = tokens.shape
    return pl.pallas_call(
        functools.partial(attention_back_kernel, nblk=nblk, where=where),
        grid=(rows,),
        in_specs=[SMEM, per_row(length, D), per_row(length, 3 * D), per_row(length, D), per_row(length, D), whole((D, 3 * D))],
        out_specs=[per_row(length, D), whole((D, 3 * D)), whole((8, D))],
        out_shape=[
            jax.ShapeDtypeStruct((rows, length, D), BF),
            jax.ShapeDtypeStruct((D, 3 * D), BF),
            jax.ShapeDtypeStruct((8, D), F32),
        ],
        scratch_shapes=[pltpu.VMEM((rows * length, D), BF), pltpu.VMEM((rows * length, 3 * D), BF)],
        compiler_params=pltpu.CompilerParams(vmem_limit_bytes=VMEM_LIMIT),
        name="attention_back",
    )(lengths, tokens, packed, grad_mixed, grad_first_in, w_in)


def pieces_of(array, me, nblk):
    rows = array.shape[0] // nblk
    return [lax.dynamic_slice_in_dim(array, (me ^ k) * rows, rows, axis=0) for k in range(nblk)]


def swap(pieces, nblk):
    return [pieces[0]] + [
        lax.ppermute(pieces[k], "blk", [(i, i ^ k) for i in range(nblk)]) for k in range(1, nblk)
    ]


def placed(pieces, me, nblk):
    rows = pieces[0].shape[0]
    out = jnp.zeros((rows * nblk,) + pieces[0].shape[1:], pieces[0].dtype)
    for k in range(nblk):
        out = lax.dynamic_update_slice_in_dim(out, pieces[k], (me ^ k) * rows, axis=0)
    return out


def to_rows(array, me, nblk):
    return jnp.concatenate(swap(pieces_of(array, me, nblk), nblk), axis=1)


def to_blocks(array, me, nblk):
    block = array.shape[1] // nblk
    return placed(swap([array[:, k * block : (k + 1) * block] for k in range(nblk)], nblk), me, nblk)


def on_device(
    tokens,
    lengths,
    input_weight,
    query_bias,
    value_bias,
    output_weight,
    output_bias,
    first_gain,
    first_shift,
    up_weight,
    up_bias,
    down_weight,
    down_bias,
    second_gain,
    second_shift,
    out_grad,
    pool_grad,
):
    batch, block, _ = tokens.shape
    nblk = lax.axis_size("blk")
    me = lax.axis_index("blk")
    rows = batch // nblk
    row = lambda v: v.reshape(1, -1)
    bias = row(jnp.concatenate([query_bias, jnp.zeros_like(query_bias), value_bias]))
    x = to_rows(tokens, me, nblk)
    out_grad = to_rows(out_grad, me, nblk)
    own_lengths = lax.dynamic_slice_in_dim(lengths, me * rows, rows, axis=0)
    own_pool = lax.dynamic_slice_in_dim(pool_grad, me * rows, rows, axis=0)
    packed, mixed, first_in = attention_forward(
        own_lengths, x, input_weight, bias, output_weight, row(output_bias), nblk
    )
    hidden, pooled, slope, grad_second, down_grad, vec2 = feed_forward(
        own_lengths, first_in, up_weight, row(up_bias), down_weight, row(down_bias), row(first_gain),
        row(first_shift), row(second_gain), row(second_shift), out_grad, own_pool, nblk,
    )
    grad_first_in, grad_mixed, up_grad, output_grad, vec1, up_bias_grad = feed_back(
        first_in, slope, grad_second, mixed, up_weight, down_weight, output_weight, row(first_gain),
        row(first_shift),
    )
    tokens_grad, input_grad, vec0 = attention_back(
        own_lengths, x, packed, grad_mixed, grad_first_in, input_weight, nblk
    )
    axes = ("rows", "blk")
    total = lambda a: lax.psum(a, axes).astype(F32)
    vecs = lax.psum(jnp.concatenate([vec0[:2], vec1[:3], vec2[:3], up_bias_grad.reshape(-1, D)], axis=0), axes)
    return (
        to_blocks(hidden, me, nblk),
        lax.all_gather(pooled, "blk", axis=0, tiled=True),
        to_blocks(tokens_grad, me, nblk).astype(F32),
        total(input_grad),
        vecs[0],
        vecs[1],
        total(output_grad),
        vecs[4],
        vecs[2],
        vecs[3],
        total(up_grad),
        vecs[8:].reshape(-1),
        total(down_grad),
        vecs[7],
        vecs[5],
        vecs[6],
    )


def solution(mesh):
    whole_rows = P("rows", "blk", None)
    rest = (P(),) * 13
    return jax.shard_map(
        on_device,
        mesh=mesh,
        in_specs=(whole_rows, P("rows", None)) + rest + (whole_rows, P("rows", None, None)),
        out_specs=(whole_rows, P("rows", None, None), whole_rows) + rest,
        check_vma=False,
    )
```

time: 987 us -> 445 us (0.45)
  matrix products: 358 us -> 0 us
  waiting for transfers between devices: 456 us -> 181 us
  Pallas kernels: 0 us -> 121 us
  local copies, waits for them, and re-layouts: 90.6 us -> 11.7 us
  blocking collectives: 42.9 us -> 76.9 us
    dot_general x19 -> x0, matrix products: 340 us -> none  [the longest x1 81.6 us: on_device(): jnp.einsum('bhqk,bqhe->bkhe', grad_scores, query_heads, preferred_element...]
    psum x2 -> x1, waiting for transfers between devices: 398 us -> 156 us  [on_device(): total = lambda a: lax.psum(a, axes).astype(F32)]
    pallas_call x0 -> x4, Pallas kernels: none -> 121 us  [the longest x1 38.2 us: attention_back(): pl.pallas_call(functools.partial(attention_back_kernel, nblk=nblk, where=...]
    all_gather x2 -> x0, waiting for transfers between devices: 57.1 us -> none  [the longest x1 35 us: on_device(): lax.all_gather(key_block, 'blk', axis=1, tiled=True)]
    unnamed x91 -> x43, local copies, waits for them, and re-layouts: 38.6 us -> 0.78 us
    all_gather x0 -> x1, blocking collectives: none -> 34.1 us  [on_device(): lax.all_gather(pooled, 'blk', axis=0, tiled=True)]
    ppermute x0 -> x12, waiting for transfers between devices: none -> 24.9 us  [swap(): lax.ppermute(pieces[k], 'blk', [(i, i ^ k) for i in range(nblk)])]
    convert_element_type x4 -> x0, local copies, waits for them, and re-layouts: 21.3 us -> none  [the longest x1 8.73 us: on_device(): key_gradient.reshape(batch, length, width).astype(jnp.bfloat16)]
  transfers between devices with their start and end apart: 6 -> 13, of which waited for: 4 -> 4; matrix products, arithmetic and copies ran while one was open for 21% -> 3% of each run, Pallas kernels for 0% -> 4%
where the time goes in v1:
time: 445 us; the launch traced here: 438 us
  waiting for transfers between devices  181 us (41%)
  Pallas kernels  121 us (27%)
  blocking collectives  76.9 us (17%)
  other arithmetic  22.2 us (5%)
  between operations  14.7 us (3%)
  local copies, waits for them, and re-layouts  11.7 us (3%)
  starting transfers between devices  10.6 us (2%)
    psum x1, waiting for transfers between devices, on_device(): total = lambda a: lax.psum(a, axes).astype(F32)  156 us
    psum x1, blocking collectives, on_device(): lax.psum(jnp.concatenate([vec0[:2], vec1[:3], vec2[:3], up_bias_grad.resh...  42.8 us
    pallas_call x1, Pallas kernels, attention_back(): pl.pallas_call(functools.partial(attention_back_kernel, nblk=nblk, where=...  38.2 us
    all_gather x1, blocking collectives, on_device(): lax.all_gather(pooled, 'blk', axis=0, tiled=True)  34.1 us
    pallas_call x1, Pallas kernels, feed_forward(): pl.pallas_call(functools.partial(feed_forward_kernel, nblk=nblk, where=wh...  33.3 us
    pallas_call x1, Pallas kernels, feed_back(): pl.pallas_call(feed_back_kernel, grid=(rows,), in_specs=[per_row(length,...  31.5 us
    ppermute x12, waiting for transfers between devices, swap(): lax.ppermute(pieces[k], 'blk', [(i, i ^ k) for i in range(nblk)])  24.9 us
    pallas_call x1, Pallas kernels, attention_forward(): pl.pallas_call(functools.partial(attention_kernel, nblk=nblk, where=where...  18.3 us
  transfers between devices with their start and end apart: 13, of which 4 were waited for; matrix products, arithmetic and copies ran while one was open for 3% of the time, Pallas kernels for 4%

profile of v1, /device:TPU:0, one launch (start us, length us, event | category | flops | bytes accessed | tf_op | source)
XLA Modules:
  0.0 438.3 jit_solution(10226702549807336149)
XLA Ops:
  7.3 1.6 constant_dynamic-slice_fusion.8
  9.4 2.6 collective-permute-start.1
  12.5 1.9 collective-permute-start.4
  18.6 1.3 constant_dynamic-slice_fusion.9.lengths_ref
  20.4 1.5 collective-permute-done.1
  21.9 7.9 %collective-permute-done.2 = bf16[2,128,768]{2,1,0:T(8,128)(2,1)S(1)} collective-permute-done((bf16[2,128,768]{2,1,0:T(8,128)(2,1)S(1)}, bf16[2,128,768]{2,1,0:T(8,128)(2,1)S(1)}, u32[]{:S(2)}, u32[]{:S(2)}) %collective-permute-start.2) | collective-permute-done | bytes 393248 | tf_op jit(solution)/shard_map/ppermute | solution.py:387
  29.8 1.2 pad_maximum_fusion.tokens_ref
  31.1 18.3 %attention_forward.1 = (bf16[2,512,2304]{2,1,0:T(8,128)(2,1)}, bf16[2,512,768]{2,1,0:T(8,128)(2,1)}, f32[2,512,768]{2,1,0:T(8,128)}) custom-call(s32[2,8]{1,0:T(2,128)} %constant_dynamic-slice_fusion.9.lengths_ref, bf16[2,512,768]{2,1,0:T(8,128)(2,1)} %pad_maximum_fusion.tokens_ref, bf16[768,2304]{1,0:T(8,128)(2,1)} %w_in_ref.3, ...), custom_call_target="tpu_custom_call" | custom-call | tf_op jit(solution)/shard_map/attention_forward/pallas_call | solution.py:121
  49.4 1.3 pad_maximum_fusion.1.out_grad_ref
  50.7 33.3 %feed_forward.1 = (bf16[2,512,768]{2,1,0:T(8,128)(2,1)}, f32[2,8,768]{2,1,0:T(8,128)}, bf16[2,512,3072]{2,1,0:T(8,128)(2,1)}, f32[2,512,768]{2,1,0:T(8,128)}, bf...) custom-call(s32[2,8]{1,0:T(2,128)} %constant_dynamic-slice_fusion.9.lengths_ref, ...), custom_call_target="tpu_custom_call" | custom-call | tf_op jit(solution)/shard_map/feed_forward/pallas_call | solution.py:211
  84.0 31.5 %feed_back.1 = (f32[2,512,768]{2,1,0:T(8,128)}, bf16[2,512,768]{2,1,0:T(8,128)(2,1)}, bf16[768,3072]{1,0:T(8,128)(2,1)}, bf16[768,768]{1,0:T(8,128)(2,1)}, f32[8,768]{1,0:T(8,128)}, /*index=5*/f32[1,3072]{1,0:T(1,128)}) custom-call(f32[2,512,768]{2,1,0:T(8,128)} %get-tuple-element.34.first_in_ref, bf16[2,512,3072]{2,1,0:T(8,128)(2,1)} %get-tuple-element.38.slope_ref, ...), custom_call_target="tpu_custom_call" | custom-call | tf_op jit(solution)/shard_map/feed_back/pallas_call | solution.py:278
  115.5 38.2 %attention_back.1 = (bf16[2,512,768]{2,1,0:T(8,128)(2,1)}, bf16[768,2304]{1,0:T(8,128)(2,1)}, f32[8,768]{1,0:T(8,128)}) custom-call(s32[2,8]{1,0:T(2,128)} %constant_dynamic-slice_fusion.9.lengths_ref, bf16[2,512,768]{2,1,0:T(8,128)(2,1)} %pad_maximum_fusion.tokens_ref, bf16[2,512,2304]{2,1,0:T(8,128)(2,1)} %get-tuple-element.37.packed_ref, ...), custom_call_target="tpu_custom_call" | custom-call | tf_op jit(solution)/shard_map/attention_back/pallas_call | solution.py:364
  153.8 0.9 slice.68
  156.0 42.8 %psum.36 = f32[12,768]{1,0:T(8,128)S(1)} all-reduce(f32[12,768]{1,0:T(8,128)S(1)} %pad_maximum_fusion.2), channel_id=1, replica_groups=mesh['rows'=8,'blk'=4] {'rows','blk'}, use_global_device_ids=true, to_apply=%region_1.0 | all-reduce | flops 9216 | bytes 73728 | tf_op jit(solution)/shard_map/psum | solution.py:453
  199.7 2.3 collective-permute-start.10
  202.6 1.9 collective-permute-start.7
  205.2 34.1 %all_gather.3 = f32[8,8,768]{2,1,0:T(8,128)S(1)} all-gather(f32[2,8,768]{2,1,0:T(8,128)S(1)} %copy-done.9), channel_id=1, replica_groups=mesh['rows'=8,'blk'=4] {'blk'}, dimensions={0}, use_global_device_ids=true | all-gather | bytes 245760 | tf_op jit(solution)/shard_map/all_gather | solution.py:456
  240.1 1.9 convert_element_type.15
  242.1 15.4 %collective-permute-done.8 = bf16[2,128,768]{2,1,0:T(8,128)(2,1)S(1)} collective-permute-done((bf16[2,128,768]{2,1,0:T(8,128)(2,1)S(1)}, bf16[2,128,768]{2,1,0:T(8,128)(2,1)S(1)}, u32[]{:S(2)}, u32[]{:S(2)}) %collective-permute-start.8) | collective-permute-done | bytes 393248 | tf_op jit(solution)/shard_map/ppermute | solution.py:387
  257.6 155.9 %all-reduce.3.cloned.1.call-done = (bf16[768,2304]{1,0:T(8,128)(2,1)}, bf16[768,768]{1,0:T(8,128)(2,1)}, bf16[768,3072]{1,0:T(8,128)(2,1)}, bf16[3072,768]{1,0:T(8,128)(2,1)}) async-done(((bf16[768,2304]{1,0:T(8,128)(2,1)}, bf16[768,768]{1,0:T(8,128)(2,1)}, bf16[768,3072]{1,0:T(8,128)(2,1)}, bf16[3072,768]{1,0:T(8,128)(2,1)}), (bf16[768,2304]{1,0:T(8,128)(2,1)}, bf16[768,768]{1,0:T(8,128)(2,1)}, ...) | async-done | bytes 14155792 | tf_op jit(solution)/shard_map/psum | solution.py:452
  413.5 7.5 %convert_element_type.18 = f32[768,3072]{1,0:T(8,128)} convert(bf16[768,3072]{1,0:T(8,128)(2,1)} %get-tuple-element.62) | non-fusion elementwise | flops 2359296 | bytes 14155776 | tf_op jit(solution)/shard_map/convert_element_type | solution.py:452
  421.0 4.5 %convert_element_type.19 = f32[3072,768]{1,0:T(8,128)} convert(bf16[3072,768]{1,0:T(8,128)(2,1)S(1)} %copy-done.2) | non-fusion elementwise | flops 2359296 | bytes 14155776 | tf_op jit(solution)/shard_map/convert_element_type | solution.py:452
  425.5 3.5 convert_element_type.16
  429.0 1.6 convert_element_type.17
  (92 shorter events, 10.6 us)
Async XLA Ops:
  7.2 12.6 %copy-start = (bf16[8,8,768]{2,1,0:T(8,128)(2,1)S(1)}, bf16[8,8,768]{2,1,0:T(8,128)(2,1)}, u32[]{:S(2)}) copy-start(bf16[8,8,768]{2,1,0:T(8,128)(2,1)} %param.33) | copy-start | bytes 294916
  7.2 406.3 %all-reduce.3.cloned.1.call-start = ((), (), s32[]{:S(2)}) async-start(), calls=%async_computation | async-start | bytes 28311552 | tf_op jit(solution)/shard_map/psum | solution.py:452
  7.3 4.9 %copy-start.5 = (bf16[8,128,768]{2,1,0:T(8,128)(2,1)S(1)}, bf16[8,128,768]{2,1,0:T(8,128)(2,1)}, u32[]{:S(2)}) copy-start(bf16[8,128,768]{2,1,0:T(8,128)(2,1)} %param.32) | copy-start | bytes 4718596
  8.9 5.6 %collective-permute-start = (bf16[2,128,768]{2,1,0:T(8,128)(2,1)S(1)}, bf16[2,128,768]{2,1,0:T(8,128)(2,1)S(1)}, u32[]{:S(2)}, u32[]{:S(2)}) collective-permute-start(bf16[2,128,768]{2,1,0:T(8,128)(2,1)S(1)} %get-tuple-element.77), channel_id=1, source_target_pairs={{0,1},{1,0},{2,3},{3,2},{4,5},{5,4},{6,7},{7,6},{8,9},{9,8},{10,11... | collective-permute-start | bytes 1179656 | tf_op jit(solution)/shard_map/ppermute | solution.py:387
  9.4 12.6 %collective-permute-start.1 = (bf16[2,128,768]{2,1,0:T(8,128)(2,1)S(1)}, bf16[2,128,768]{2,1,0:T(8,128)(2,1)S(1)}, u32[]{:S(2)}, u32[]{:S(2)}) collective-permute-start(bf16[2,128,768]{2,1,0:T(8,128)(2,1)S(1)} %get-tuple-element.79), channel_id=1, source_target_pairs={{0,2},{1,3},{2,0},{3,1},{4,6},{5,7},{6,4},{7,5},{8,10},{9,11},{10,... | collective-permute-start | bytes 1179656 | tf_op jit(solution)/shard_map/ppermute | solution.py:387
  12.0 3.7 copy-start.14
  12.0 4.3 copy-start.15
  12.0 4.8 %copy-start.16 = (f32[768]{0:T(1024)S(1)}, f32[768]{0:T(1024)}, u32[]{:S(2)}) copy-start(f32[768]{0:T(1024)} %param.29) | copy-start | bytes 9220
  12.0 5.4 %copy-start.17 = (f32[768]{0:T(1024)S(1)}, f32[768]{0:T(1024)}, u32[]{:S(2)}) copy-start(f32[768]{0:T(1024)} %param.30) | copy-start | bytes 9220
  12.0 6.0 %copy-start.18 = (f32[768]{0:T(1024)S(1)}, f32[768]{0:T(1024)}, u32[]{:S(2)}) copy-start(f32[768]{0:T(1024)} %param.31) | copy-start | bytes 9220
  12.0 17.8 %collective-permute-start.2 = (bf16[2,128,768]{2,1,0:T(8,128)(2,1)S(1)}, bf16[2,128,768]{2,1,0:T(8,128)(2,1)S(1)}, u32[]{:S(2)}, u32[]{:S(2)}) collective-permute-start(bf16[2,128,768]{2,1,0:T(8,128)(2,1)S(1)} %get-tuple-element.78), channel_id=1, source_target_pairs={{0,3},{1,2},{2,1},{3,0},{4,7},{5,6},{6,5},{7,4},{8,11},{9,10},{10,... | collective-permute-start | bytes 1179656 | tf_op jit(solution)/shard_map/ppermute | solution.py:387
  12.3 37.1 %collective-permute-start.3 = (bf16[2,128,768]{2,1,0:T(8,128)(2,1)S(1)}, bf16[2,128,768]{2,1,0:T(8,128)(2,1)S(1)}, u32[]{:S(2)}, u32[]{:S(2)}) collective-permute-start(bf16[2,128,768]{2,1,0:T(8,128)(2,1)S(1)} %get-tuple-element.73), channel_id=1, source_target_pairs={{0,1},{1,0},{2,3},{3,2},{4,5},{5,4},{6,7},{7,6},{8,9},{9,8},{10,11... | collective-permute-start | bytes 1179656 | tf_op jit(solution)/shard_map/ppermute | solution.py:387
  12.5 36.9 %collective-permute-start.4 = (bf16[2,128,768]{2,1,0:T(8,128)(2,1)S(1)}, bf16[2,128,768]{2,1,0:T(8,128)(2,1)S(1)}, u32[]{:S(2)}, u32[]{:S(2)}) collective-permute-start(bf16[2,128,768]{2,1,0:T(8,128)(2,1)S(1)} %get-tuple-element.75), channel_id=1, source_target_pairs={{0,2},{1,3},{2,0},{3,1},{4,6},{5,7},{6,4},{7,5},{8,10},{9,11},{10,... | collective-permute-start | bytes 1179656 | tf_op jit(solution)/shard_map/ppermute | solution.py:387
  14.4 35.0 %collective-permute-start.5 = (bf16[2,128,768]{2,1,0:T(8,128)(2,1)S(1)}, bf16[2,128,768]{2,1,0:T(8,128)(2,1)S(1)}, u32[]{:S(2)}, u32[]{:S(2)}) collective-permute-start(bf16[2,128,768]{2,1,0:T(8,128)(2,1)S(1)} %get-tuple-element.74), channel_id=1, source_target_pairs={{0,3},{1,2},{2,1},{3,0},{4,7},{5,6},{6,5},{7,4},{8,11},{9,10},{10,... | collective-permute-start | bytes 1179656 | tf_op jit(solution)/shard_map/ppermute | solution.py:387
  153.8 45.7 %copy-start.7 = (bf16[2,512,768]{2,1,0:T(8,128)(2,1)S(1)}, bf16[2,512,768]{2,1,0:T(8,128)(2,1)}, u32[]{:S(2)}) copy-start(bf16[2,512,768]{2,1,0:T(8,128)(2,1)} %get-tuple-element.43) | copy-start | bytes 4718596
  199.7 39.7 %collective-permute-start.9 = (bf16[2,128,768]{2,1,0:T(8,128)(2,1)S(1)}, bf16[2,128,768]{2,1,0:T(8,128)(2,1)S(1)}, u32[]{:S(2)}, u32[]{:S(2)}) collective-permute-start(bf16[2,128,768]{2,1,0:T(8,128)(2,1)S(1)} %get-tuple-element.66), channel_id=1, source_target_pairs={{0,1},{1,0},{2,3},{3,2},{4,5},{5,4},{6,7},{7,6},{8,9},{9,8},{10,11... | collective-permute-start | bytes 1179656 | tf_op jit(solution)/shard_map/ppermute | solution.py:387
  199.7 40.2 %collective-permute-start.10 = (bf16[2,128,768]{2,1,0:T(8,128)(2,1)S(1)}, bf16[2,128,768]{2,1,0:T(8,128)(2,1)S(1)}, u32[]{:S(2)}, u32[]{:S(2)}) collective-permute-start(bf16[2,128,768]{2,1,0:T(8,128)(2,1)S(1)} %get-tuple-element.65), channel_id=1, source_target_pairs={{0,2},{1,3},{2,0},{3,1},{4,6},{5,7},{6,4},{7,5},{8,10},{9,11},{10,... | collective-permute-start | bytes 1179656 | tf_op jit(solution)/shard_map/ppermute | solution.py:387
  202.1 37.9 %collective-permute-start.11 = (bf16[2,128,768]{2,1,0:T(8,128)(2,1)S(1)}, bf16[2,128,768]{2,1,0:T(8,128)(2,1)S(1)}, u32[]{:S(2)}, u32[]{:S(2)}) collective-permute-start(bf16[2,128,768]{2,1,0:T(8,128)(2,1)S(1)} %get-tuple-element.64), channel_id=1, source_target_pairs={{0,3},{1,2},{2,1},{3,0},{4,7},{5,6},{6,5},{7,4},{8,11},{9,10},{10,... | collective-permute-start | bytes 1179656 | tf_op jit(solution)/shard_map/ppermute | solution.py:387
  202.4 39.6 %collective-permute-start.6 = (bf16[2,128,768]{2,1,0:T(8,128)(2,1)S(1)}, bf16[2,128,768]{2,1,0:T(8,128)(2,1)S(1)}, u32[]{:S(2)}, u32[]{:S(2)}) collective-permute-start(bf16[2,128,768]{2,1,0:T(8,128)(2,1)S(1)} %get-tuple-element.70), channel_id=1, source_target_pairs={{0,1},{1,0},{2,3},{3,2},{4,5},{5,4},{6,7},{7,6},{8,9},{9,8},{10,11... | collective-permute-start | bytes 1179656 | tf_op jit(solution)/shard_map/ppermute | solution.py:387
  202.6 39.4 %collective-permute-start.7 = (bf16[2,128,768]{2,1,0:T(8,128)(2,1)S(1)}, bf16[2,128,768]{2,1,0:T(8,128)(2,1)S(1)}, u32[]{:S(2)}, u32[]{:S(2)}) collective-permute-start(bf16[2,128,768]{2,1,0:T(8,128)(2,1)S(1)} %get-tuple-element.69), channel_id=1, source_target_pairs={{0,2},{1,3},{2,0},{3,1},{4,6},{5,7},{6,4},{7,5},{8,10},{9,11},{10,... | collective-permute-start | bytes 1179656 | tf_op jit(solution)/shard_map/ppermute | solution.py:387
  239.3 18.2 %collective-permute-start.8 = (bf16[2,128,768]{2,1,0:T(8,128)(2,1)S(1)}, bf16[2,128,768]{2,1,0:T(8,128)(2,1)S(1)}, u32[]{:S(2)}, u32[]{:S(2)}) collective-permute-start(bf16[2,128,768]{2,1,0:T(8,128)(2,1)S(1)} %get-tuple-element.68), channel_id=1, source_target_pairs={{0,3},{1,2},{2,1},{3,0},{4,7},{5,6},{6,5},{7,4},{8,11},{9,10},{10,... | collective-permute-start | bytes 1179656 | tf_op jit(solution)/shard_map/ppermute | solution.py:387
  257.6 163.4 %copy-start.4 = (bf16[8,128,768]{2,1,0:T(8,128)(2,1)}, bf16[8,128,768]{2,1,0:T(8,128)(2,1)S(1)}, u32[]{:S(2)}) copy-start(bf16[8,128,768]{2,1,0:T(8,128)(2,1)S(1)} %constant_dynamic-update-slice_fusion.3) | copy-start | bytes 4718596
  413.5 7.5 %copy-start.2 = (bf16[3072,768]{1,0:T(8,128)(2,1)S(1)}, bf16[3072,768]{1,0:T(8,128)(2,1)}, u32[]{:S(2)}) copy-start(bf16[3072,768]{1,0:T(8,128)(2,1)} %get-tuple-element.63) | copy-start | bytes 14155780
  421.0 4.5 %copy-start.3 = (bf16[768,2304]{1,0:T(8,128)(2,1)S(1)}, bf16[768,2304]{1,0:T(8,128)(2,1)}, u32[]{:S(2)}) copy-start(bf16[768,2304]{1,0:T(8,128)(2,1)} %get-tuple-element.60) | copy-start | bytes 10616836
  (10 other events, 25.0 us)
Sparse Core Ops, SparseCore 0:
  154.0 259.4 all-reduce.2

commit v2 on v1

v2 whole, which is shorter than its diff:
```python
import functools
import jax
import jax.numpy as jnp
from jax import lax
from jax.experimental import pallas as pl
from jax.experimental.pallas import tpu as pltpu
from jax.sharding import PartitionSpec as P

D = 768
H = 12
DH = 64
FF = 3072
NSEG = 8
PAIR = 2 * DH
NORM_EPS = 1e-12
BIG = 1e9
BF = jnp.bfloat16
F32 = jnp.float32
CHUNK = 512
VMEM_LIMIT = 60 * 1024 * 1024


def nn(a, b):
    return lax.dot_general(a, b, (((1,), (0,)), ((), ())), preferred_element_type=F32)


def nt(a, b):
    return lax.dot_general(a, b, (((1,), (1,)), ((), ())), preferred_element_type=F32)


def tn(a, b):
    return lax.dot_general(a, b, (((0,), (0,)), ((), ())), preferred_element_type=F32)


def col_sum(a):
    return jnp.sum(a, axis=0, keepdims=True)


def norm_parts(hidden):
    center = hidden - jnp.mean(hidden, axis=-1, keepdims=True)
    spread = jnp.mean(center * center, axis=-1, keepdims=True)
    inverse = lax.rsqrt(spread + NORM_EPS)
    return center * inverse, inverse


def norm_back(grad, gain, unit, inverse):
    scaled = grad * gain
    along = jnp.mean(scaled * unit, axis=-1, keepdims=True)
    return inverse * (scaled - jnp.mean(scaled, axis=-1, keepdims=True) - unit * along)


def segments(lengths_ref, row, length, count, nblk, me, first=0):
    shape = (count, PAIR)
    local = lax.broadcasted_iota(jnp.int32, shape, 0) + first
    block = length // nblk
    places = ((local // block) ^ me) * block + local % block
    end = jnp.int32(0)
    labels = jnp.zeros(shape, jnp.int32)
    for c in range(NSEG):
        end = end + lengths_ref[row, c]
        labels = labels + (places >= end).astype(jnp.int32)
    return labels == lax.broadcasted_iota(jnp.int32, shape, 1)


def head_masks(length):
    lane = lax.broadcasted_iota(jnp.int32, (length, PAIR), 1)
    return lane < DH, lane >= DH


PLACE = {"y": 0, "x": 1, "a": 2, "b": 3}
BLOCKS = 16
DOWN_ORDER = ("xyab", "yxab", 3)
UP_ORDER = ("xyab", "yxab", 3)
HEAD_ORDER = ("xyab", "yxab", 3)
TAIL = "duhrtdurvudrvurvdrv1durv2u34r5r6"


def own_place():
    blk = lax.axis_index("blk")
    rows = lax.axis_index("rows")
    return blk & 1, ((rows & 7) << 1) | ((blk >> 1) & 1), blk


def slot_in(order, halved, block, here):
    slot = 0
    for t, bit in enumerate(order):
        at = block ^ here if t < halved else block
        slot = slot | (((at >> PLACE[bit]) & 1) << (3 - t))
    return slot


def slot_of(orders, core, block, here):
    return jnp.where(
        core == 0, slot_in(orders[0], orders[2], block, here), slot_in(orders[1], orders[2], block, here)
    )


def hand_out(slots_ref, send_ref, keep_ref, sems):
    half = BLOCKS // 2
    copies = [
        pltpu.make_async_copy(slots_ref.at[pl.ds(half, half)], send_ref, sems.at[0]),
        pltpu.make_async_copy(slots_ref.at[pl.ds(0, half)], keep_ref, sems.at[1]),
    ]
    for c in copies:
        c.start()
    for c in copies:
        c.wait()


def whole(shape):
    return pl.BlockSpec(shape, lambda *_: (0,) * len(shape), pipeline_mode=pl.Buffered(1))


def per_row(*shape):
    return pl.BlockSpec((1,) + shape, lambda r: (r,) + (0,) * len(shape))


def flat(*shape):
    return pl.BlockSpec(shape, lambda r: (r,) + (0,) * (len(shape) - 1))


SMEM = pl.BlockSpec(memory_space=pltpu.SMEM)
ANY = pl.BlockSpec(memory_space=pl.ANY)


def slots(rows, cols):
    half = (ANY, (BLOCKS // 2, rows, cols), BF)
    return [half, half], [pltpu.VMEM((BLOCKS, rows, cols), BF), pltpu.SemaphoreType.DMA((2,))]


def shape_of(shape, dtype):
    return jax.ShapeDtypeStruct(shape, dtype)


def call(kernel, name, grid, in_specs, outs, scratch=(), flops=0, nbytes=0, aliases=None):
    return pl.pallas_call(
        kernel,
        grid=grid,
        in_specs=in_specs,
        out_specs=[o[0] for o in outs],
        out_shape=[shape_of(o[1], o[2]) for o in outs],
        scratch_shapes=scratch,
        input_output_aliases=aliases or {},
        compiler_params=pltpu.CompilerParams(vmem_limit_bytes=VMEM_LIMIT),
        cost_estimate=pl.CostEstimate(flops=int(flops), bytes_accessed=int(nbytes), transcendentals=0),
        name=name,
    )


def attention_kernel(lengths_ref, *refs, nblk, place):
    pieces = refs[:nblk]
    w_in_ref, bias_ref, w_out_ref, out_bias_ref, x_ref, packed_ref, mixed_ref, first_in_ref = refs[nblk:]
    block = pieces[0].shape[1]
    length = block * nblk
    for i in range(nblk):
        x_ref[pl.ds(i * block, block), :] = pieces[i][0]
    x = x_ref[...]
    for c in range(3):
        cols = pl.ds(c * D, D)
        packed_ref[0, :, cols] = (nn(x, w_in_ref[:, cols]) + bias_ref[:, cols]).astype(BF)
    hit = segments(lengths_ref, pl.program_id(0), length, length, nblk, place()[2])
    here = jnp.where(hit, 1.0, 0.0).astype(BF)
    away = jnp.where(hit, 0.0, -BIG).astype(BF)
    masks = head_masks(length)
    for j in range(H // 2):
        q = packed_ref[0, :, pl.ds(j * PAIR, PAIR)] * jnp.asarray(DH**-0.5, BF)
        k = packed_ref[0, :, pl.ds(D + j * PAIR, PAIR)]
        v = packed_ref[0, :, pl.ds(2 * D + j * PAIR, PAIR)]
        k_aug = jnp.concatenate([k, away], axis=1)
        outs = []
        for h in range(2):
            qh = jnp.where(masks[h], q, jnp.zeros_like(q))
            s = nt(jnp.concatenate([qh, here], axis=1), k_aug)
            e = jnp.exp(s - jnp.max(s, axis=1, keepdims=True))
            total = jnp.sum(e, axis=1, keepdims=True)
            outs.append(nn(e.astype(BF), v) / total)
        mixed_ref[:, pl.ds(j * PAIR, PAIR)] = jnp.where(masks[0], outs[0], outs[1]).astype(BF)
    branch = nn(mixed_ref[...], w_out_ref[...]) + out_bias_ref[...]
    first_in_ref[...] = x.astype(F32) + branch


def attention_forward(lengths, pieces, w_in, bias, w_out, out_bias, place=own_place):
    nblk = len(pieces)
    rows, block, _ = pieces[0].shape
    length = block * nblk
    return call(
        functools.partial(attention_kernel, nblk=nblk, place=place),
        "attention_forward",
        (rows,),
        [SMEM] + [per_row(block, D)] * nblk + [whole((D, 3 * D)), whole((1, 3 * D)), whole((D, D)), whole((1, D))],
        [
            (flat(length, D), (rows * length, D), BF),
            (per_row(length, 3 * D), (rows, length, 3 * D), BF),
            (flat(length, D), (rows * length, D), BF),
            (flat(length, D), (rows * length, D), F32),
        ],
        flops=18e9,
    )(lengths, *pieces, w_in, bias, w_out, out_bias)


def gelu_both(x):
    cdf = 0.5 + 0.5 * lax.erf(x * (0.5**0.5))
    density = jnp.exp(x * x * -0.5) * 0.3989422804014327
    return x * cdf, cdf + x * density


def feed_kernel(lengths_ref, first_in_ref, pool_grad_ref, *refs, nblk, place):
    grad_pieces = refs[:nblk]
    (w_up_ref, up_bias_ref, w_down_ref, down_bias_ref, w_out_ref, g1_ref, b1_ref, g2_ref, b2_ref) = refs[nblk : nblk + 9]
    hidden = refs[nblk + 9 : 2 * nblk + 9]
    (low_ref, active_own_ref, active_other_ref, inner_own_ref, inner_other_ref, grad_first_in_ref, grad_mixed_ref,
     branch_own_ref, branch_other_ref, vec_ref, up_sums_ref,
     active_ref, slope_ref, inner_ref, branch_ref, pooled_ref) = refs[2 * nblk + 9 :]
    step = pl.program_id(0)
    r, part = step // 2, step % 2
    count = first_in_ref.shape[0]
    block = hidden[0].shape[1] - 2 * NSEG
    length = block * nblk
    some = nblk // 2
    half = FF // 2
    core, _, blk = place()
    own = pl.ds(pl.multiple_of(core * half, 128), half)
    other = pl.ds(pl.multiple_of((core ^ 1) * half, 128), half)

    unit1, inverse1 = norm_parts(first_in_ref[...])
    first = unit1 * g1_ref[...] + b1_ref[...]
    low = first.astype(BF)
    low_ref[...] = low
    acc = first + down_bias_ref[...]
    for c in range(FF // CHUNK):
        cols = pl.ds(c * CHUNK, CHUNK)
        inner = nn(low, w_up_ref[:, cols]) + up_bias_ref[:, cols]
        act, slope = gelu_both(inner)
        act = act.astype(BF)
        active_ref[:, cols] = act
        slope_ref[:, cols] = slope.astype(BF)
        acc = acc + nn(act, w_down_ref[cols, :])
    active_own_ref[...] = active_ref[:, own]
    active_other_ref[:, :half] = active_ref[:, other]
    unit, inverse = norm_parts(acc)
    result = unit * g2_ref[...] + b2_ref[...]
    high = result.astype(BF)
    here = jnp.where(segments(lengths_ref, r, length, count, nblk, blk, part * count), 1.0, 0.0).astype(BF)
    rest = (result - high.astype(F32)).astype(BF)
    sums = (tn(here, high) + tn(here, rest))[:NSEG]
    sub = lax.broadcasted_iota(jnp.int32, (NSEG, 1), 0)
    counts = jnp.zeros((NSEG, 1), F32)
    for c in range(NSEG):
        counts = jnp.where(sub == c, lengths_ref[r, c].astype(F32), counts)

    @pl.when(part == 0)
    def _():
        pooled_ref[...] = sums
        for i in range(some):
            hidden[i][0, :block, :] = high[i * block : (i + 1) * block]

    @pl.when(part == 1)
    def _():
        pooled = (pooled_ref[...] + sums) / counts
        pooled_high = pooled.astype(BF)
        both = jnp.concatenate([pooled_high.astype(F32), pooled - pooled_high.astype(F32)], axis=0).astype(BF)
        for i in range(some):
            hidden[some + i][0, :block, :] = high[i * block : (i + 1) * block]
        for i in range(nblk):
            hidden[i][0, block:, :] = both

    share = pool_grad_ref[0].astype(F32) / counts
    share_high = share.astype(BF)
    share_rest = (share - share_high.astype(F32)).astype(BF)
    pad = jnp.zeros((PAIR - NSEG, D), BF)
    spread = nn(here, jnp.concatenate([share_high, pad], axis=0)) + nn(here, jnp.concatenate([share_rest, pad], axis=0))
    given = jnp.where(
        part == 0,
        jnp.concatenate([g[0] for g in grad_pieces[:some]], axis=0).astype(F32),
        jnp.concatenate([g[0] for g in grad_pieces[some:]], axis=0).astype(F32),
    )
    grad = given + spread
    acc = norm_back(grad, g2_ref[...], unit, inverse)
    outer = acc.astype(BF)
    active_other_ref[:, half:] = outer
    sums2 = [col_sum(grad * unit), col_sum(grad), col_sum(outer.astype(F32))]
    bias_sums = []
    for c in range(FF // CHUNK):
        cols = pl.ds(c * CHUNK, CHUNK)
        inner = (nt(outer, w_down_ref[cols, :]) * slope_ref[:, cols].astype(F32)).astype(BF)
        inner_ref[:, cols] = inner
        bias_sums.append(col_sum(inner.astype(F32)))
        acc = acc + nt(inner, w_up_ref[:, cols])
    inner_own_ref[...] = inner_ref[:, own]
    inner_other_ref[...] = inner_ref[:, other]
    grad_first_in = norm_back(acc, g1_ref[...], unit1, inverse1)
    grad_first_in_ref[...] = grad_first_in
    branch = grad_first_in.astype(BF)
    branch_ref[...] = branch
    for ref, flip in ((branch_own_ref, 0), (branch_other_ref, 1)):
        ref[...] = branch_ref[:, pl.ds(pl.multiple_of((core ^ flip) * (D // 2), 128), D // 2)]
    grad_mixed_ref[...] = nt(branch, w_out_ref[...]).astype(BF)
    sums1 = [col_sum(acc * unit1), col_sum(acc), col_sum(branch.astype(F32))]
    vec = jnp.concatenate(sums1 + sums2 + [jnp.zeros((2, D), F32)], axis=0)
    up_sums = jnp.concatenate([jnp.concatenate(bias_sums, axis=1), jnp.zeros((7, FF), F32)], axis=0)

    @pl.when(step == 0)
    def _():
        vec_ref[...] = vec
        up_sums_ref[...] = up_sums

    @pl.when(step != 0)
    def _():
        vec_ref[...] += vec
        up_sums_ref[...] += up_sums


def feed(lengths, first_in, pool_grad, grads, w_up, up_bias, w_down, down_bias, w_out, g1, b1, g2, b2, place=own_place):
    nblk = len(grads)
    rows, block, _ = grads[0].shape
    total = first_in.shape[0]
    tile = block * nblk // 2
    vec = whole((1, D))

    def row(*shape):
        return pl.BlockSpec((1,) + shape, lambda i: (i // 2,) + (0,) * len(shape))

    def out(cols, dtype=BF):
        return flat(tile, cols), (total, cols), dtype

    half = FF // 2
    return call(
        functools.partial(feed_kernel, nblk=nblk, place=place),
        "feed",
        (total // tile,),
        [SMEM, flat(tile, D), row(NSEG, D)] + [row(block, D)] * nblk
        + [whole((D, FF)), whole((1, FF)), whole((FF, D)), vec, whole((D, D)), vec, vec, vec, vec],
        [(row(block + 2 * NSEG, D), (rows, block + 2 * NSEG, D), BF)] * nblk
        + [out(D), out(half), out(half + D), out(half), out(half), out(D, F32), out(D), out(D // 2), out(D // 2),
           (whole((8, D)), (8, D), F32), (whole((8, FF)), (8, FF), F32)],
        scratch=[pltpu.VMEM((tile, FF), BF)] * 3 + [pltpu.VMEM((tile, D), BF), pltpu.VMEM((NSEG, D), F32)],
        flops=40e9,
    )(lengths, first_in, pool_grad, *grads, w_up, up_bias, w_down, down_bias, w_out, g1, b1, g2, b2)


def down_kernel(
    active_ref, outer_ref, came_active_ref, came_outer_ref, send_ref, keep_ref, slots_ref, sems, place, orders
):
    step = pl.program_id(0)
    core, here_block, _ = place()
    rows = slots_ref.shape[1]
    here = active_ref.shape[1] // rows
    tile = (tn(active_ref[...], outer_ref[...]) + tn(came_active_ref[...], came_outer_ref[...])).astype(BF)
    for i in range(here):
        slots_ref[slot_of(orders, core, step * here + i, here_block)] = tile[i * rows : (i + 1) * rows]

    @pl.when(step == pl.num_programs(0) - 1)
    def _():
        hand_out(slots_ref, send_ref, keep_ref, sems)


def down_gradient(active, mine, came, orders, place=own_place):
    total, half = active.shape
    outs, scratch = slots(half // BLOCKS, D)
    wide = 384
    part = pl.BlockSpec((total, wide), lambda j: (0, j))
    outer = pl.BlockSpec((total, D), lambda j: (0, half // D), pipeline_mode=pl.Buffered(1))
    return call(
        functools.partial(down_kernel, place=place, orders=orders),
        "down_gradient",
        (half // wide,),
        [part, outer, part, outer],
        outs,
        scratch=scratch,
        flops=6e9,
    )(active, mine, came, came)


def up_kernel(low_ref, inner_ref, came_low_ref, came_inner_ref, send_ref, keep_ref, slots_ref, sems, place, orders):
    step = pl.program_id(0)
    core, here_block, _ = place()
    rows = slots_ref.shape[1]
    wide = inner_ref.shape[1]
    tile = (tn(low_ref[...], inner_ref[...]) + tn(came_low_ref[...], came_inner_ref[...])).astype(BF)
    cols = pl.ds(pl.multiple_of(step * wide, 128), wide)
    for i in range(BLOCKS):
        slots_ref[slot_of(orders, core, i, here_block), :, cols] = tile[i * rows : (i + 1) * rows]

    @pl.when(step == pl.num_programs(0) - 1)
    def _():
        hand_out(slots_ref, send_ref, keep_ref, sems)


def up_gradient(low, inner, came_low, came_inner, orders, place=own_place):
    total, half = inner.shape
    outs, scratch = slots(D // BLOCKS, half)
    wide = 512
    part = pl.BlockSpec((total, wide), lambda j: (0, j))
    return call(
        functools.partial(up_kernel, place=place, orders=orders),
        "up_gradient",
        (half // wide,),
        [whole((total, D)), part, whole((total, D)), part],
        outs,
        scratch=scratch,
        flops=6e9,
    )(low, inner, came_low, came_inner)


def attention_back_kernel(lengths_ref, *refs, nblk, place):
    q_ref, k_ref, v_ref, gm_ref, grads_ref, other_ref, vec_ref = refs
    r = pl.program_id(0)
    core, _, blk = place()
    length = q_ref.shape[1]
    wide = 3 * PAIR
    hit = segments(lengths_ref, r, length, length, nblk, blk)
    here = jnp.where(hit, 1.0, 0.0).astype(BF)
    away = jnp.where(hit, 0.0, -BIG).astype(BF)
    masks = head_masks(length)
    scale = DH**-0.5
    for j in range(2):
        lanes = slice(j * PAIR, (j + 1) * PAIR)
        q = q_ref[0, :, lanes] * jnp.asarray(scale, BF)
        k = k_ref[0, :, lanes]
        v = v_ref[0, :, lanes]
        gm = gm_ref[:, lanes]
        k_aug = jnp.concatenate([k, away], axis=1)
        zero = jnp.zeros_like(q)
        gq = gk = gv = 0.0
        for h in range(2):
            qh = jnp.where(masks[h], q, zero)
            kh = jnp.where(masks[h], k, zero)
            gmh = jnp.where(masks[h], gm, zero)
            s = nt(k_aug, jnp.concatenate([qh, here], axis=1))
            e = jnp.exp(s - jnp.max(s, axis=0, keepdims=True))
            p = e * (1.0 / jnp.sum(e, axis=0, keepdims=True))
            gp = nt(v, gmh)
            delta = jnp.sum(gp * p, axis=0, keepdims=True)
            gs = (p * (gp - delta)).astype(BF)
            gv = gv + nn(p.astype(BF), gmh)
            gk = gk + nn(gs, qh)
            gq = gq + tn(gs, kh)
        grads = jnp.concatenate([(gq * scale).astype(BF), gk.astype(BF), gv.astype(BF)], axis=1)
        at = pl.ds(j * wide, wide)
        grads_ref[:, at] = grads
        sums = jnp.concatenate([col_sum(grads.astype(F32)), jnp.zeros((7, wide), F32)], axis=0)

        @pl.when(r == 0)
        def _():
            vec_ref[:, at] = sums

        @pl.when(r != 0)
        def _():
            vec_ref[:, at] += sums

    other_ref[...] = grads_ref[:, pl.ds(pl.multiple_of((core ^ 1) * wide, 128), wide)]


def attention_back(lengths, packed, grad_mixed, nblk, group, place=own_place):
    rows, length, _ = packed.shape
    total = rows * length

    def pairs(section):
        return pl.BlockSpec((1, length, 2 * PAIR), lambda r: (r, 0, section * (H // 4) + group))

    return call(
        functools.partial(attention_back_kernel, nblk=nblk, place=place),
        "attention_back",
        (rows,),
        [SMEM, pairs(0), pairs(1), pairs(2), pl.BlockSpec((length, 2 * PAIR), lambda r: (r, group))],
        [(flat(length, D), (total, D), BF), (flat(length, D // 2), (total, D // 2), BF), (whole((8, D)), (8, D), F32)],
        flops=12e9,
    )(lengths, packed, packed, packed, grad_mixed)


def head_gradient_kernel(*refs, count, place, orders):
    lefts, rights, came_rights = refs[:4], refs[4 : 4 + count], refs[4 + count : 4 + 2 * count]
    send_ref, keep_ref = refs[4 + 2 * count : 6 + 2 * count]
    held, right_held, slots_ref, sems, left_sems, right_sems = refs[6 + 2 * count :]
    core, here_block, _ = place()
    wide = D // 2
    left_loads = [pltpu.make_async_copy(ref, held.at[n], left_sems.at[n]) for n, ref in enumerate(lefts)]
    right_loads = []
    for n, ref in enumerate(rights):
        lanes = pl.ds(pl.multiple_of(core * wide, 128), wide) if ref.shape[1] == D else pl.ds(0, wide)
        right_loads.append(pltpu.make_async_copy(ref.at[:, lanes], right_held.at[n, 0], right_sems.at[2 * n]))
        right_loads.append(pltpu.make_async_copy(came_rights[n], right_held.at[n, 1], right_sems.at[2 * n + 1]))
    order = left_loads[:2] + right_loads[:2] + left_loads[2:] + right_loads[2:]
    for load in order:
        load.start()
    rows = D // BLOCKS
    for n in range(count):
        if n < 2:
            left_loads[2 * n].wait()
            left_loads[2 * n + 1].wait()
        right_loads[2 * n].wait()
        right_loads[2 * n + 1].wait()
        at = 0 if n == 0 else 2
        tile = (tn(held[at], right_held[n, 0]) + tn(held[at + 1], right_held[n, 1])).astype(BF)
        for i in range(BLOCKS):
            slot = slot_of(orders, core, i, here_block)
            slots_ref[slot, :, n * wide : (n + 1) * wide] = tile[i * rows : (i + 1) * rows]
    hand_out(slots_ref, send_ref, keep_ref, sems)


def head_gradient(lefts, rights, came_rights, orders, place=own_place):
    total = lefts[0].shape[0]
    count = len(rights)
    wide = D // 2
    outs, scratch = slots(D // BLOCKS, count * wide)
    return call(
        functools.partial(head_gradient_kernel, count=count, place=place, orders=orders),
        "head_gradient",
        (1,),
        [ANY] * (4 + 2 * count),
        outs,
        scratch=[pltpu.VMEM((4, total, D), BF), pltpu.VMEM((count, 2, total, wide), BF)] + scratch
        + [pltpu.SemaphoreType.DMA((4,)), pltpu.SemaphoreType.DMA((2 * count,))],
        flops=6e9,
    )(*lefts, *rights, *came_rights)


def tokens_grad_kernel(*refs, groups, nblk):
    grads = refs[:groups]
    grad_first_in_ref, w_in_ref = refs[groups : groups + 2]
    outs = refs[groups + 2 : groups + 2 + nblk]
    all_ref = refs[-1]
    length = grad_first_in_ref.shape[0]
    block = length // nblk
    for g in range(groups):
        for j in range(2):
            for section in range(3):
                at = section * D + (2 * g + j) * PAIR
                start = (3 * j + section) * PAIR
                all_ref[:, at : at + PAIR] = grads[g][:, start : start + PAIR]
    total = (grad_first_in_ref[...] + nt(all_ref[...], w_in_ref[...])).astype(BF)
    for i in range(nblk):
        outs[i][0] = total[i * block : (i + 1) * block]


def tokens_gradient(grads, grad_first_in, w_in, nblk, rows):
    length = grad_first_in.shape[0] // rows
    block = length // nblk
    return call(
        functools.partial(tokens_grad_kernel, groups=len(grads), nblk=nblk),
        "tokens_gradient",
        (rows,),
        [flat(length, D)] * len(grads) + [flat(length, D), whole((D, 3 * D))],
        [(per_row(block, D), (rows, block, D), BF)] * nblk,
        scratch=[pltpu.VMEM((length, 3 * D), BF)],
        flops=5e9,
    )(*grads, grad_first_in, w_in)


def place_hidden_kernel(*refs, nblk, rows, block, place):
    pieces, (hidden_ref, pooled_ref) = refs[:nblk], refs[nblk:]
    blk = place()[2]
    for i in range(nblk):
        for r in range(rows):
            at = (blk ^ i) * rows + r
            hidden_ref[pl.ds(at, 1)] = pieces[i][pl.ds(r, 1), :block, :]
            tail = pieces[i][r, block:, :].astype(F32)
            pooled_ref[pl.ds(at, 1)] = (tail[:NSEG] + tail[NSEG:]).reshape(1, NSEG, D)


def place_hidden(pieces, place=own_place):
    nblk = len(pieces)
    rows, block, _ = pieces[0].shape
    block -= 2 * NSEG
    return call(
        functools.partial(place_hidden_kernel, nblk=nblk, rows=rows, block=block, place=place),
        "place_hidden",
        (1,),
        [whole((rows, block + 2 * NSEG, D))] * nblk,
        [(whole((rows * nblk, block, D)), (rows * nblk, block, D), BF), (whole((rows * nblk, NSEG, D)), (rows * nblk, NSEG, D), F32)],
        flops=1e9,
    )(*pieces)


def place_tokens_kernel(*refs, nblk, rows, place):
    pieces, out_ref = refs[:nblk], refs[nblk]
    blk = place()[2]
    for i in range(nblk):
        for r in range(rows):
            out_ref[pl.ds((blk ^ i) * rows + r, 1)] = pieces[i][pl.ds(r, 1)].astype(F32)


def place_tokens(pieces, place=own_place):
    nblk = len(pieces)
    rows, block, _ = pieces[0].shape
    return call(
        functools.partial(place_tokens_kernel, nblk=nblk, rows=rows, place=place),
        "place_tokens",
        (1,),
        [whole((rows, block, D))] * nblk,
        [(whole((rows * nblk, block, D)), (rows * nblk, block, D), F32)],
        flops=1e9,
    )(*pieces)[0]


def unpack_kernel(half_ref, *refs, flip, place, orders):
    out_ref = refs[-1]
    core, here_block, _ = place()
    rows = half_ref.shape[1]
    count = out_ref.shape[0] // rows
    for i in range(count):
        slot = slot_of(orders, core ^ flip, pl.program_id(0) * count + i, here_block)
        out_ref[i * rows : (i + 1) * rows, :] = half_ref[slot].astype(F32)


def unpack_feed(half, by_rows, flip, before, orders, place=own_place):
    _, rows, cols = half.shape
    parts = 4
    core = lambda: place()[0] ^ flip
    tall = rows * BLOCKS
    shape, index = (
        ((2 * tall, cols), lambda q: (core() * parts + q, 0)) if by_rows else ((tall, 2 * cols), lambda q: (q, core()))
    )
    extra = [] if before is None else [before]
    return call(
        functools.partial(unpack_kernel, flip=flip, place=place, orders=orders),
        "unpack_feed",
        (parts,),
        [whole(half.shape)] + [ANY] * len(extra),
        [(pl.BlockSpec((tall // parts, cols), index), shape, F32)],
        aliases={1: 0} if extra else None,
        flops=2e9,
    )(half, *extra)[0]


def unpack_heads_kernel(half_ref, *refs, flip, place, orders):
    output_ref, input_ref = refs[-2:]
    core, here_block, _ = place()
    rows = D // BLOCKS
    step = pl.program_id(0)

    def fill(out_ref):
        cols = pl.ds(pl.multiple_of(step * PAIR, 128), PAIR)
        for i in range(BLOCKS):
            slot = slot_of(orders, core ^ flip, i, here_block)
            out_ref[i * rows : (i + 1) * rows, :] = half_ref[slot, :, cols].astype(F32)

    @pl.when(step < 3)
    def _():
        fill(output_ref)

    @pl.when(step >= 3)
    def _():
        fill(input_ref)


def unpack_heads(half, flip, before, orders, place=own_place):
    core = lambda: place()[0] ^ flip

    def input_index(j):
        k = jnp.maximum(j - 3, 0)
        return 0, (k % 3) * (H // 2) + 2 * (k // 3) + core()

    extra = [] if before is None else list(before)
    return call(
        functools.partial(unpack_heads_kernel, flip=flip, place=place, orders=orders),
        "unpack_heads",
        (half.shape[2] // PAIR,),
        [whole(half.shape)] + [ANY] * len(extra),
        [
            (pl.BlockSpec((D, PAIR), lambda j: (0, core() * 3 + jnp.minimum(j, 2))), (D, D), F32),
            (pl.BlockSpec((D, PAIR), input_index), (D, 3 * D), F32),
        ],
        aliases={1: 0, 2: 1} if extra else None,
        flops=2e9,
    )(half, *extra)


def exchange(array, bits):
    nblk, nrows = lax.axis_size("blk"), lax.axis_size("rows")
    moves = {"c": (0, 1), "y": (0, 2), "x": (1, 0), "a": (2, 0), "b": (4, 0)}
    pairs = []
    for i in range(nblk * nrows):
        row, blk = divmod(i, nblk)
        bit = bits[blk & 1]
        by_row, by_blk = moves[bit] if isinstance(bit, str) else (bit, 0)
        pairs.append((i, (row ^ by_row) * nblk + (blk ^ by_blk)))
    return lax.ppermute(array, ("rows", "blk"), pairs)


def added(left, right):
    return (left.astype(F32) + right.astype(F32)).astype(BF)


class Sum:
    def __init__(self, send, keep, orders):
        self.keep = keep
        extra = []
        bit = 8
        while bit < lax.axis_size("rows"):
            extra.append(bit)
            bit *= 2
        bits = [(orders[0][t], orders[1][t]) for t in range(4)]
        halves, wholes = bits[: orders[2]], bits[orders[2] :]
        self.plan = [("half", h) for h in halves] + [("all", w) for w in wholes] + [("all", (e, e)) for e in extra]
        self.plan += [("join", h) for h in reversed(halves)] + [("end", ("c", "c"))]
        self.moving = exchange(send, self.plan[0][1])
        self.stage = 0

    def busy(self):
        return self.stage < len(self.plan)

    def step(self, marks=()):
        if not self.busy():
            return []
        kind = self.plan[self.stage][0]
        (came,) = after([self.moving], marks)
        self.stage += 1
        if kind == "end":
            self.other = came
            return [self.other]
        if kind == "half":
            if self.plan[self.stage][0] == "half":
                n = self.keep.shape[0] // 2
                send, self.keep = added(self.keep[n:], came[n:]), added(self.keep[:n], came[:n])
            else:
                send = self.now = added(self.keep, came)
        elif kind == "all":
            send = self.now = added(self.now, came)
        else:
            send = self.now = jnp.concatenate([self.now, came], axis=0)
        self.moving = exchange(send, self.plan[self.stage][1])
        return [send]

    def last(self):
        return self.stage == len(self.plan) - 1


class Vectors:
    def __init__(self, value):
        self.value = value
        bit = 8
        self.left = ["c", "y", "x", "a", "b"]
        while bit < lax.axis_size("rows"):
            self.left.append(bit)
            bit *= 2

    def step(self, marks=()):
        if self.left:
            bit = self.left.pop(0)
            (here,) = after([self.value], marks)
            self.value = here + exchange(here, (bit, bit))
        return [self.value]

    def finish(self):
        while self.left:
            self.step()
        return self.value


def after(arrays, *marks):
    marks = [m for mark in marks for m in mark]
    return list(lax.optimization_barrier(tuple(arrays) + tuple(marks))[: len(arrays)])


def pieces_of(array, me, nblk):
    rows = array.shape[0] // nblk
    return [lax.dynamic_slice_in_dim(array, (me ^ k) * rows, rows, axis=0) for k in range(nblk)]


def swap(pieces):
    nblk = len(pieces)
    return [pieces[0]] + [
        lax.ppermute(pieces[k], "blk", [(i, i ^ k) for i in range(nblk)]) for k in range(1, nblk)
    ]


def on_device(
    tokens,
    lengths,
    input_weight,
    query_bias,
    value_bias,
    output_weight,
    output_bias,
    first_gain,
    first_shift,
    up_weight,
    up_bias,
    down_weight,
    down_bias,
    second_gain,
    second_shift,
    out_grad,
    pool_grad,
):
    nblk = lax.axis_size("blk")
    me = lax.axis_index("blk")
    rows = tokens.shape[0] // nblk
    row = lambda v: v.reshape(1, -1)
    g1, b1 = row(first_gain), row(first_shift)
    bias = row(jnp.concatenate([query_bias, jnp.zeros_like(query_bias), value_bias]))
    own_lengths = lax.dynamic_slice_in_dim(lengths, me * rows, rows, axis=0)
    own_pool = lax.dynamic_slice_in_dim(pool_grad, me * rows, rows, axis=0)
    pieces = swap(pieces_of(tokens, me, nblk))
    grads = swap(pieces_of(out_grad, me, nblk))
    twin = lambda a: exchange(a, ("c", "c"))
    x, packed, mixed, first_in = attention_forward(
        own_lengths, pieces, input_weight, bias, output_weight, row(output_bias)
    )
    came_x, came_mixed = twin(x), twin(mixed)
    *hidden, low, active, active_outer, inner, inner_other, grad_first_in, grad_mixed, branch, branch_other, vec1, ups = feed(
        own_lengths, first_in, own_pool, grads, up_weight, row(up_bias), down_weight, row(down_bias), output_weight,
        g1, b1, row(second_gain), row(second_shift),
    )
    came_active = twin(active_outer)
    came_low, came_inner, came_branch = twin(low), twin(inner_other), twin(branch_other)
    hidden = swap(hidden)

    def attention(group, marks):
        grad_packed, other, sums = attention_back(own_lengths, packed, after([grad_mixed], marks)[0], nblk, group)
        return grad_packed, twin(other), sums[0].reshape(2, 3, PAIR)

    gp0, came0, vec_a = attention(0, [])
    active, came_active = after([active, came_active], [gp0])
    send, keep = down_gradient(active, active_outer, came_active, DOWN_ORDER)
    down = Sum(send, keep, DOWN_ORDER)
    (inner,) = after([inner], [keep])
    send, keep = up_gradient(low, inner, came_low, came_inner, UP_ORDER)
    up = Sum(send, keep, UP_ORDER)
    gp1, came1, vec_b = attention(1, [keep] + hidden)
    m = down.step([gp1])
    gp2, came2, vec_c = attention(2, m)
    m = up.step(down.step([gp2]))
    (mixed,) = after([mixed], m)
    send, keep = head_gradient(
        [mixed, came_mixed, x, came_x], [branch, gp0, gp1, gp2], [came_branch, came0, came1, came2], HEAD_ORDER
    )
    heads = Sum(send, keep, HEAD_ORDER)
    m = up.step(down.step([keep]))
    sections = jnp.concatenate([vec_a, vec_b, vec_c], axis=0)
    vecs = Vectors(
        jnp.concatenate(
            [sections[:, 0].reshape(1, D), sections[:, 2].reshape(1, D), vec1[:6], ups[0].reshape(-1, D)], axis=0
        )
    )
    gp0, gp1, gp2, vecs.value = after([gp0, gp1, gp2, vecs.value], m)
    tokens_pieces = tokens_gradient([gp0, gp1, gp2], grad_first_in, input_weight, nblk, rows)
    tokens_grad = swap(tokens_pieces)
    m = tokens_pieces[:1]
    sums = {"d": down, "u": up, "r": heads, "v": vecs}
    held = {"down": None, "up": None, "heads": None}
    for action in TAIL:
        if action in sums:
            m = sums[action].step(m)
        elif action == "h":
            hidden_out, pooled = place_hidden(after(hidden, m))
            m = [hidden_out]
        elif action == "t":
            tokens_out = place_tokens(after(tokens_grad, m))
            m = [tokens_out]
        else:
            which, flip = divmod(int(action) - 1, 2)
            total = (down, up, heads)[which]
            while not total.last() and total.busy() or (flip and total.busy()):
                m = total.step(m)
            (half,) = after([total.other if flip else total.now], m)
            if which == 0:
                held["down"] = unpack_feed(half, True, flip, held["down"], DOWN_ORDER)
                m = [held["down"]]
            elif which == 1:
                held["up"] = unpack_feed(half, False, flip, held["up"], UP_ORDER)
                m = [held["up"]]
            else:
                held["heads"] = unpack_heads(half, flip, held["heads"], HEAD_ORDER)
                m = held["heads"]
    down_grad, up_grad, (output_grad, input_grad) = held["down"], held["up"], held["heads"]
    vecs = vecs.finish()
    return (
        hidden_out,
        pooled,
        tokens_out,
        input_grad,
        vecs[0],
        vecs[1],
        output_grad,
        vecs[4],
        vecs[2],
        vecs[3],
        up_grad,
        vecs[8:12].reshape(-1),
        down_grad,
        vecs[7],
        vecs[5],
        vecs[6],
    )


def solution(mesh):
    whole_rows = P("rows", "blk", None)
    rest = (P(),) * 13
    return jax.shard_map(
        on_device,
        mesh=mesh,
        in_specs=(whole_rows, P("rows", None)) + rest + (whole_rows, P("rows", None, None)),
        out_specs=(whole_rows, P("rows", None, None), whole_rows) + rest,
        check_vma=False,
    )
```

time: 445 us -> 349 us (0.78)
  waiting for transfers between devices: 181 us -> 86.2 us
  blocking collectives: 76.9 us -> 0 us
  Pallas kernels: 121 us -> 179 us
  starting transfers between devices: 10.6 us -> 40.9 us
  between operations: 14.7 us -> 1.46 us
  local copies, waits for them, and re-layouts: 11.7 us -> 19.7 us
  other arithmetic: 22.2 us -> 14.7 us
    psum x1 -> x0, waiting for transfers between devices: 156 us -> none  [on_device(): total = lambda a: lax.psum(a, axes).astype(F32)]
    ppermute x0 -> x38, waiting for transfers between devices: none -> 69.6 us  [exchange(): return lax.ppermute(array, ('rows', 'blk'), pairs)]
    pallas_call x4 -> x17, Pallas kernels: 121 us -> 179 us  [the longest x1 46.7 us: feed(): call(functools.partial(feed_kernel, nblk=nblk, place=place), 'feed', (tot...]
    psum x1 -> x0, blocking collectives: 42.8 us -> none  [on_device(): lax.psum(jnp.concatenate([vec0[:2], vec1[:3], vec2[:3], up_bias_grad.resh...]
    all_gather x1 -> x0, blocking collectives: 34.1 us -> none  [on_device(): lax.all_gather(pooled, 'blk', axis=0, tiled=True)]
    ppermute x0 -> x38, starting transfers between devices: none -> 31.2 us  [exchange(): return lax.ppermute(array, ('rows', 'blk'), pairs)]
    convert_element_type x5 -> x12, other arithmetic: 19 us -> 7.81 us  [added(): return (left.astype(F32) + right.astype(F32)).astype(BF)]
    ppermute x12, waiting for transfers between devices: 24.9 us -> 16.6 us  [swap(): lax.ppermute(pieces[k], 'blk', [(i, i ^ k) for i in range(nblk)])]
  transfers between devices with their start and end apart: 13 -> 50, of which waited for: 4 -> 17; matrix products, arithmetic and copies ran while one was open for 3% -> 7% of each run, Pallas kernels for 4% -> 37%
where the time goes in v2:
time: 349 us; the launch traced here: 342 us
  Pallas kernels  179 us (51%)
  waiting for transfers between devices  86.2 us (25%)
  starting transfers between devices  40.9 us (12%)
  local copies, waits for them, and re-layouts  19.7 us (6%)
  other arithmetic  14.7 us (4%)
    ppermute x38, waiting for transfers between devices, exchange(): return lax.ppermute(array, ('rows', 'blk'), pairs)  69.6 us
    pallas_call x1, Pallas kernels, feed(): call(functools.partial(feed_kernel, nblk=nblk, place=place), 'feed', (tot...  46.7 us
    pallas_call x3, Pallas kernels, attention_back(): call(functools.partial(attention_back_kernel, nblk=nblk, place=place), 'a...  37.4 us
    ppermute x38, starting transfers between devices, exchange(): return lax.ppermute(array, ('rows', 'blk'), pairs)  31.2 us
    pallas_call x1, Pallas kernels, attention_forward(): call(functools.partial(attention_kernel, nblk=nblk, place=place), 'attent...  17.7 us
    pallas_call x4, Pallas kernels, unpack_feed(): call(functools.partial(unpack_kernel, flip=flip, place=place, orders=orde...  17 us
    ppermute x12, waiting for transfers between devices, swap(): lax.ppermute(pieces[k], 'blk', [(i, i ^ k) for i in range(nblk)])  16.6 us
    pallas_call x2, Pallas kernels, unpack_heads(): call(functools.partial(unpack_heads_kernel, flip=flip, place=place, order...  14.1 us
  transfers between devices with their start and end apart: 50, of which 17 were waited for; matrix products, arithmetic and copies ran while one was open for 7% of the time, Pallas kernels for 37%

profile of v2, /device:TPU:0, one launch (start us, length us, event | category | flops | bytes accessed | tf_op | source)
XLA Modules:
  0.0 341.8 jit_solution(3639571442667517630)
XLA Ops:
  16.0 8.1 %collective-permute-done.2.refs_3_ = bf16[2,128,768]{2,1,0:T(8,128)(2,1)S(1)} collective-permute-done((bf16[2,128,768]{2,1,0:T(8,128)(2,1)S(1)}, bf16[2,128,768]{2,1,0:T(8,128)(2,1)S(1)}, u32[]{:S(2)}, u32[]{:S(2)}) %collective-permute-start.2) | collective-permute-done | bytes 393248 | tf_op jit(solution)/shard_map/ppermute | solution.py:764
  24.8 17.7 %attention_forward.1 = (bf16[1024,768]{1,0:T(8,128)(2,1)}, bf16[2,512,2304]{2,1,0:T(8,128)(2,1)}, bf16[1024,768]{1,0:T(8,128)(2,1)}, f32[1024,768]{1,0:T(8,128)}) custom-call(s32[2,8]{1,0:T(2,128)} %constant_dynamic-slice_fusion.9.lengths_ref, bf16[2,128,768]{2,1,0:T(8,128)(2,1)} %get-tuple-element.228.refs_0_, bf16[2,128,768]{2,1,0:T(8,128)(2,1)} %copy-done.30, ...), custom_call_target="tpu_custom_call" | custom-call | flops 17999998976 | tf_op jit(solution)/shard_map/attention_forward/pallas_call | solution.py:186
  43.5 46.7 %feed.1 = (bf16[2,144,768]{2,1,0:T(8,128)(2,1)}, bf16[2,144,768]{2,1,0:T(8,128)(2,1)}, bf16[2,144,768]{2,1,0:T(8,128)(2,1)}, bf16[2,144,768]{2,1,0:T(8,128)(2,1)...) custom-call(s32[2,8]{1,0:T(2,128)} %constant_dynamic-slice_fusion.9., ...), custom_call_target="tpu_custom_call" | custom-call | flops 40000000000 | tf_op jit(solution)/shard_map/feed/pallas_call | solution.py:327
  94.4 12.7 %attention_back.3 = (bf16[1024,768]{1,0:T(8,128)(2,1)}, bf16[1024,384]{1,0:T(8,128)(2,1)}, f32[8,768]{1,0:T(8,128)}) custom-call(s32[2,8]{1,0:T(2,128)} %constant_dynamic-slice_fusion.9.lengths_ref, bf16[2,512,2304]{2,1,0:T(8,128)(2,1)} %get-tuple-element.121.refs_0_.refs_1_.refs_2_, bf16[2,512,2304]{2,1,0:T(8,128)(2,1)} %get-tuple-element.121.refs_0_.refs_1_.refs_2_, ...), custom_call_target="tpu_custom_call" | custom-call | flops 12000000000 | tf_op jit(solution)/shard_map/attention_back/pallas_call | solution.py:461
  108.1 9.6 %down_gradient.1 = (bf16[8,96,768]{2,1,0:T(8,128)(2,1)}, bf16[8,96,768]{2,1,0:T(8,128)(2,1)}) custom-call(bf16[1024,1536]{1,0:T(8,128)(2,1)} %get-tuple-element.124.active_ref, bf16[1024,2304]{1,0:T(8,128)(2,1)} %get-tuple-element.120.outer_ref, bf16[1024,2304]{1,0:T(8,128)(2,1)} %collective-permute-done.9.came_active_ref.came_outer_ref, ...), custom_call_target="tpu_custom_call" | custom-call | flops 6000000000 | tf_op jit(solution)/shard_map/down_gradient/pallas_call | solution.py:363
  119.8 9.4 %up_gradient.1 = (bf16[8,48,1536]{2,1,0:T(8,128)(2,1)}, bf16[8,48,1536]{2,1,0:T(8,128)(2,1)}) custom-call(bf16[1024,768]{1,0:T(8,128)(2,1)} %get-tuple-element.117.low_ref, bf16[1024,1536]{1,0:T(8,128)(2,1)} %get-tuple-element.127.inner_ref, bf16[1024,768]{1,0:T(8,128)(2,1)} %collective-permute-done.10.came_low_ref, bf16[1024,1536]{1,0:T(8,128)(2,1)} %copy-done.23), custom_call_target="tpu_custom_call" | custom-call | flops 6000000000 | tf_op jit(solution)/shard_map/up_gradient/pallas_call | solution.py:394
  131.5 12.4 %attention_back.4 = (bf16[1024,768]{1,0:T(8,128)(2,1)}, bf16[1024,384]{1,0:T(8,128)(2,1)}, f32[8,768]{1,0:T(8,128)}) custom-call(s32[2,8]{1,0:T(2,128)} %constant_dynamic-slice_fusion.9.lengths_ref, bf16[2,512,2304]{2,1,0:T(8,128)(2,1)} %get-tuple-element.121.refs_0_.refs_1_.refs_2_, bf16[2,512,2304]{2,1,0:T(8,128)(2,1)} %get-tuple-element.121.refs_0_.refs_1_.refs_2_, ...), custom_call_target="tpu_custom_call" | custom-call | flops 12000000000 | tf_op jit(solution)/shard_map/attention_back/pallas_call | solution.py:461
  144.8 13.8 %collective-permute-done.13 = bf16[8,96,768]{2,1,0:T(8,128)(2,1)S(1)} collective-permute-done((bf16[8,96,768]{2,1,0:T(8,128)(2,1)}, bf16[8,96,768]{2,1,0:T(8,128)(2,1)S(1)}, u32[]{:S(2)}, u32[]{:S(2)}) %collective-permute-start.13) | collective-permute-done | bytes 1179680 | tf_op jit(solution)/shard_map/ppermute | solution.py:678
  161.6 12.3 %attention_back.5 = (bf16[1024,768]{1,0:T(8,128)(2,1)}, bf16[1024,384]{1,0:T(8,128)(2,1)}, f32[8,768]{1,0:T(8,128)}) custom-call(s32[2,8]{1,0:T(2,128)} %constant_dynamic-slice_fusion.9.lengths_ref, bf16[2,512,2304]{2,1,0:T(8,128)(2,1)} %get-tuple-element.121.refs_0_.refs_1_.refs_2_, bf16[2,512,2304]{2,1,0:T(8,128)(2,1)} %get-tuple-element.121.refs_0_.refs_1_.refs_2_, ...), custom_call_target="tpu_custom_call" | custom-call | flops 12000000000 | tf_op jit(solution)/shard_map/attention_back/pallas_call | solution.py:461
  181.8 11.9 %head_gradient.1 = (bf16[8,48,1536]{2,1,0:T(8,128)(2,1)}, bf16[8,48,1536]{2,1,0:T(8,128)(2,1)}) custom-call(bf16[1024,768]{1,0:T(8,128)(2,1)} %get-tuple-element.140.refs_0_, bf16[1024,768]{1,0:T(8,128)(2,1)} %collective-permute-done.17.refs_1_, bf16[1024,768]{1,0:T(8,128)(2,1)} %get-tuple-element.141.refs_2_, ...), custom_call_target="tpu_custom_call" | custom-call | flops 6000000000 | tf_op jit(solution)/shard_map/head_gradient/pallas_call | solution.py:506
  199.6 8.8 %tokens_gradient.1 = (bf16[2,128,768]{2,1,0:T(8,128)(2,1)}, bf16[2,128,768]{2,1,0:T(8,128)(2,1)}, bf16[2,128,768]{2,1,0:T(8,128)(2,1)}, bf16[2,128,768]{2,1,0:T(8,128)(2,1)}) custom-call(bf16[1024,768]{1,0:T(8,128)(2,1)} %get-tuple-element.155.refs_5_.refs_0_, bf16[1024,768]{1,0:T(8,128)(2,1)} %get-tuple-element.156.refs_6_.refs_1_, ...), custom_call_target="tpu_custom_call" | custom-call | flops 5000000000 | tf_op jit(solution)/shard_map/tokens_gradient/pallas_call | solution.py:539
  223.1 7.7 %collective-permute-done.27.refs_3_ = bf16[2,128,768]{2,1,0:T(8,128)(2,1)} collective-permute-done((bf16[2,128,768]{2,1,0:T(8,128)(2,1)}, bf16[2,128,768]{2,1,0:T(8,128)(2,1)}, u32[]{:S(2)}, u32[]{:S(2)}) %collective-permute-start.27) | collective-permute-done | bytes 393248 | tf_op jit(solution)/shard_map/ppermute | solution.py:764
  239.0 7.7 %collective-permute-done.34 = bf16[2,48,1536]{2,1,0:T(8,128)(2,1)S(1)} collective-permute-done((bf16[2,48,1536]{2,1,0:T(8,128)(2,1)S(1)}, bf16[2,48,1536]{2,1,0:T(8,128)(2,1)S(1)}, u32[]{:S(2)}, u32[]{:S(2)}) %collective-permute-start.34) | collective-permute-done | bytes 294944 | tf_op jit(solution)/shard_map/ppermute | solution.py:678
  254.6 9.5 %collective-permute-done.38 = f32[12,768]{1,0:T(8,128)S(1)} collective-permute-done((f32[12,768]{1,0:T(8,128)S(1)}, f32[12,768]{1,0:T(8,128)S(1)}, u32[]{:S(2)}, u32[]{:S(2)}) %collective-permute-start.38) | collective-permute-done | bytes 36896 | tf_op jit(solution)/shard_map/ppermute | solution.py:678
  274.8 9.0 %collective-permute-done.39 = bf16[2,48,1536]{2,1,0:T(8,128)(2,1)S(1)} collective-permute-done((bf16[2,48,1536]{2,1,0:T(8,128)(2,1)S(1)}, bf16[2,48,1536]{2,1,0:T(8,128)(2,1)S(1)}, u32[]{:S(2)}, u32[]{:S(2)}) %collective-permute-start.39) | collective-permute-done | bytes 294944 | tf_op jit(solution)/shard_map/ppermute | solution.py:678
  285.0 3.8 %collective-permute-done.45 = f32[12,768]{1,0:T(8,128)S(1)} collective-permute-done((f32[12,768]{1,0:T(8,128)S(1)}, f32[12,768]{1,0:T(8,128)S(1)}, u32[]{:S(2)}, u32[]{:S(2)}) %collective-permute-start.45) | collective-permute-done | bytes 36896 | tf_op jit(solution)/shard_map/ppermute | solution.py:678
  288.8 4.3 %unpack_feed.4.refs_0_ = f32[3072,768]{1,0:T(8,128)} custom-call(bf16[16,96,768]{2,1,0:T(8,128)(2,1)} %copy-done.3), custom_call_target="tpu_custom_call" | custom-call | flops 2000000000 | tf_op jit(solution)/shard_map/unpack_feed/pallas_call | solution.py:615
  295.3 9.5 %collective-permute-done.42 = bf16[4,48,1536]{2,1,0:T(8,128)(2,1)S(1)} collective-permute-done((bf16[4,48,1536]{2,1,0:T(8,128)(2,1)S(1)}, bf16[4,48,1536]{2,1,0:T(8,128)(2,1)S(1)}, u32[]{:S(2)}, u32[]{:S(2)}) %collective-permute-start.42) | collective-permute-done | bytes 589856 | tf_op jit(solution)/shard_map/ppermute | solution.py:678
  307.9 3.7 %collective-permute-done.48 = f32[12,768]{1,0:T(8,128)S(1)} collective-permute-done((f32[12,768]{1,0:T(8,128)S(1)}, f32[12,768]{1,0:T(8,128)S(1)}, u32[]{:S(2)}, u32[]{:S(2)}) %collective-permute-start.48) | collective-permute-done | bytes 36896 | tf_op jit(solution)/shard_map/ppermute | solution.py:678
  311.6 4.3 %unpack_feed.5 = f32[3072,768]{1,0:T(8,128)} custom-call(bf16[16,96,768]{2,1,0:T(8,128)(2,1)} %collective-permute-done.44.half_ref, f32[3072,768]{1,0:T(8,128)} %unpack_feed.4.refs_0_), custom_call_target="tpu_custom_call", output_to_operand_aliasing={{}: (1, {})} | custom-call | flops 2000000000 | tf_op jit(solution)/shard_map/unpack_feed/pallas_call | solution.py:615
  315.9 4.3 %unpack_feed.6.refs_0_ = f32[768,3072]{1,0:T(8,128)} custom-call(bf16[16,48,1536]{2,1,0:T(8,128)(2,1)} %copy-done.2), custom_call_target="tpu_custom_call" | custom-call | flops 2000000000 | tf_op jit(solution)/shard_map/unpack_feed/pallas_call | solution.py:615
  320.2 4.2 %unpack_feed.7 = f32[768,3072]{1,0:T(8,128)} custom-call(bf16[16,48,1536]{2,1,0:T(8,128)(2,1)} %collective-permute-done.47.half_ref, f32[768,3072]{1,0:T(8,128)} %unpack_feed.6.refs_0_), custom_call_target="tpu_custom_call", output_to_operand_aliasing={{}: (1, {})} | custom-call | flops 2000000000 | tf_op jit(solution)/shard_map/unpack_feed/pallas_call | solution.py:615
  327.4 7.0 %unpack_heads.2 = (f32[768,768]{1,0:T(8,128)}, f32[768,2304]{1,0:T(8,128)}) custom-call(bf16[16,48,1536]{2,1,0:T(8,128)(2,1)} %copy-done.5), custom_call_target="tpu_custom_call" | custom-call | flops 2000000000 | tf_op jit(solution)/shard_map/unpack_heads/pallas_call | solution.py:655
  334.5 7.1 %unpack_heads.3 = (f32[768,768]{1,0:T(8,128)}, f32[768,2304]{1,0:T(8,128)}) custom-call(bf16[16,48,1536]{2,1,0:T(8,128)(2,1)} %collective-permute-done.49.half_ref, f32[768,768]{1,0:T(8,128)} %get-tuple-element.203.refs_0_, f32[768,2304]{1,0:T(8,128)} %get-tuple-element.204.refs_1_), custom_call_target="tpu_custom_call", output_to_operand_aliasing={{0}: (1, {}), {1}: (2, {})} | custom-call | flops 2000000000 | tf_op jit(solution)/shard_map/unpack_heads/pallas_call | solution.py:655
  (216 shorter events, 94.8 us)
Async XLA Ops:
  6.1 18.0 %collective-permute-start.2 = (bf16[2,128,768]{2,1,0:T(8,128)(2,1)S(1)}, bf16[2,128,768]{2,1,0:T(8,128)(2,1)S(1)}, u32[]{:S(2)}, u32[]{:S(2)}) collective-permute-start(bf16[2,128,768]{2,1,0:T(8,128)(2,1)S(1)} %get-tuple-element.226), channel_id=1, source_target_pairs={{0,3},{1,2},{2,1},{3,0},{4,7},{5,6},{6,5},{7,4},{8,11},{9,10},{10,... | collective-permute-start | bytes 1179656 | tf_op jit(solution)/shard_map/ppermute | solution.py:764
  7.1 35.3 %collective-permute-start.3 = (bf16[2,128,768]{2,1,0:T(8,128)(2,1)S(1)}, bf16[2,128,768]{2,1,0:T(8,128)(2,1)S(1)}, u32[]{:S(2)}, u32[]{:S(2)}) collective-permute-start(bf16[2,128,768]{2,1,0:T(8,128)(2,1)S(1)} %get-tuple-element.223), channel_id=1, source_target_pairs={{0,1},{1,0},{2,3},{3,2},{4,5},{5,4},{6,7},{7,6},{8,9},{9,8},{10,11... | collective-permute-start | bytes 1179656 | tf_op jit(solution)/shard_map/ppermute | solution.py:764
  7.3 35.2 %collective-permute-start.4 = (bf16[2,128,768]{2,1,0:T(8,128)(2,1)S(1)}, bf16[2,128,768]{2,1,0:T(8,128)(2,1)S(1)}, u32[]{:S(2)}, u32[]{:S(2)}) collective-permute-start(bf16[2,128,768]{2,1,0:T(8,128)(2,1)S(1)} %get-tuple-element.225), channel_id=1, source_target_pairs={{0,2},{1,3},{2,0},{3,1},{4,6},{5,7},{6,4},{7,5},{8,10},{9,11},{10,... | collective-permute-start | bytes 1179656 | tf_op jit(solution)/shard_map/ppermute | solution.py:764
  15.2 27.4 %collective-permute-start.5 = (bf16[2,128,768]{2,1,0:T(8,128)(2,1)S(1)}, bf16[2,128,768]{2,1,0:T(8,128)(2,1)S(1)}, u32[]{:S(2)}, u32[]{:S(2)}) collective-permute-start(bf16[2,128,768]{2,1,0:T(8,128)(2,1)S(1)} %get-tuple-element.222), channel_id=1, source_target_pairs={{0,3},{1,2},{2,1},{3,0},{4,7},{5,6},{6,5},{7,4},{8,11},{9,10},{10,... | collective-permute-start | bytes 1179656 | tf_op jit(solution)/shard_map/ppermute | solution.py:764
  91.0 27.1 %collective-permute-start.11 = (bf16[1024,1536]{1,0:T(8,128)(2,1)}, bf16[1024,1536]{1,0:T(8,128)(2,1)S(1)}, u32[]{:S(2)}, u32[]{:S(2)}) collective-permute-start(bf16[1024,1536]{1,0:T(8,128)(2,1)} %get-tuple-element.128), channel_id=1, source_target_pairs={{0,1},{1,0},{2,3},{3,2},{4,5},{5,4},{6,7},{7,6},{8,9},{9,8},{10,11... | collective-permute-start | bytes 9437192 | tf_op jit(solution)/shard_map/ppermute | solution.py:678
  91.1 38.2 %collective-permute-start.6 = (bf16[2,144,768]{2,1,0:T(8,128)(2,1)}, bf16[2,144,768]{2,1,0:T(8,128)(2,1)}, u32[]{:S(2)}, u32[]{:S(2)}) collective-permute-start(bf16[2,144,768]{2,1,0:T(8,128)(2,1)} %get-tuple-element.114), channel_id=1, source_target_pairs={{0,1},{1,0},{2,3},{3,2},{4,5},{5,4},{6,7},{7,6},{8,9},{9,8},{10,11... | collective-permute-start | bytes 1327112 | tf_op jit(solution)/shard_map/ppermute | solution.py:764
  91.5 38.0 %collective-permute-start.7 = (bf16[2,144,768]{2,1,0:T(8,128)(2,1)}, bf16[2,144,768]{2,1,0:T(8,128)(2,1)}, u32[]{:S(2)}, u32[]{:S(2)}) collective-permute-start(bf16[2,144,768]{2,1,0:T(8,128)(2,1)} %get-tuple-element.115), channel_id=1, source_target_pairs={{0,2},{1,3},{2,0},{3,1},{4,6},{5,7},{6,4},{7,5},{8,10},{9,11},{10,... | collective-permute-start | bytes 1327112 | tf_op jit(solution)/shard_map/ppermute | solution.py:764
  93.5 24.2 %collective-permute-start.10 = (bf16[1024,768]{1,0:T(8,128)(2,1)}, bf16[1024,768]{1,0:T(8,128)(2,1)}, u32[]{:S(2)}, u32[]{:S(2)}) collective-permute-start(bf16[1024,768]{1,0:T(8,128)(2,1)} %get-tuple-element.117.low_ref), channel_id=1, source_target_pairs={{0,1},{1,0},{2,3},{3,2},{4,5},{5,4},{6,7},{7,6},{8,9},{9,8},{10,11... | collective-permute-start | bytes 4718600 | tf_op jit(solution)/shard_map/ppermute | solution.py:678
  107.9 23.6 %collective-permute-start.8 = (bf16[2,144,768]{2,1,0:T(8,128)(2,1)}, bf16[2,144,768]{2,1,0:T(8,128)(2,1)S(1)}, u32[]{:S(2)}, u32[]{:S(2)}) collective-permute-start(bf16[2,144,768]{2,1,0:T(8,128)(2,1)} %get-tuple-element.116), channel_id=1, source_target_pairs={{0,3},{1,2},{2,1},{3,0},{4,7},{5,6},{6,5},{7,4},{8,11},{9,10},{10,... | collective-permute-start | bytes 1327112 | tf_op jit(solution)/shard_map/ppermute | solution.py:764
  117.7 60.3 %collective-permute-start.17 = (bf16[1024,768]{1,0:T(8,128)(2,1)}, bf16[1024,768]{1,0:T(8,128)(2,1)}, u32[]{:S(2)}, u32[]{:S(2)}) collective-permute-start(bf16[1024,768]{1,0:T(8,128)(2,1)} %get-tuple-element.140.refs_0_), channel_id=1, source_target_pairs={{0,1},{1,0},{2,3},{3,2},{4,5},{5,4},{6,7},{7,6},{8,9},{9,8},{10,11... | collective-permute-start | bytes 4718600 | tf_op jit(solution)/shard_map/ppermute | solution.py:678
  118.2 61.8 %collective-permute-start.18 = (bf16[1024,768]{1,0:T(8,128)(2,1)}, bf16[1024,768]{1,0:T(8,128)(2,1)}, u32[]{:S(2)}, u32[]{:S(2)}) collective-permute-start(bf16[1024,768]{1,0:T(8,128)(2,1)} %get-tuple-element.141.refs_2_), channel_id=1, source_target_pairs={{0,1},{1,0},{2,3},{3,2},{4,5},{5,4},{6,7},{7,6},{8,9},{9,8},{10,11... | collective-permute-start | bytes 4718600 | tf_op jit(solution)/shard_map/ppermute | solution.py:678
  129.3 45.5 %collective-permute-start.19 = (bf16[1024,384]{1,0:T(8,128)(2,1)}, bf16[1024,384]{1,0:T(8,128)(2,1)}, u32[]{:S(2)}, u32[]{:S(2)}) collective-permute-start(bf16[1024,384]{1,0:T(8,128)(2,1)} %get-tuple-element.143), channel_id=1, source_target_pairs={{0,1},{1,0},{2,3},{3,2},{4,5},{5,4},{6,7},{7,6},{8,9},{9,8},{10,11... | collective-permute-start | bytes 2359304 | tf_op jit(solution)/shard_map/ppermute | solution.py:678
  129.5 45.3 %collective-permute-start.12 = (bf16[8,48,1536]{2,1,0:T(8,128)(2,1)}, bf16[8,48,1536]{2,1,0:T(8,128)(2,1)}, u32[]{:S(2)}, u32[]{:S(2)}) collective-permute-start(bf16[8,48,1536]{2,1,0:T(8,128)(2,1)} %get-tuple-element.130), channel_id=1, source_target_pairs={{0,4},{1,3},{2,6},{3,1},{4,0},{5,7},{6,2},{7,5},{8,12},{9,11},{10,... | collective-permute-start | bytes 3538952 | tf_op jit(solution)/shard_map/ppermute | solution.py:678
  131.4 27.1 %collective-permute-start.13 = (bf16[8,96,768]{2,1,0:T(8,128)(2,1)}, bf16[8,96,768]{2,1,0:T(8,128)(2,1)S(1)}, u32[]{:S(2)}, u32[]{:S(2)}) collective-permute-start(bf16[8,96,768]{2,1,0:T(8,128)(2,1)} %get-tuple-element.131), channel_id=1, source_target_pairs={{0,4},{1,3},{2,6},{3,1},{4,0},{5,7},{6,2},{7,5},{8,12},{9,11},{10,... | collective-permute-start | bytes 3538952 | tf_op jit(solution)/shard_map/ppermute | solution.py:678
  177.9 20.2 %collective-permute-start.15 = (bf16[4,48,1536]{2,1,0:T(8,128)(2,1)S(1)}, bf16[4,48,1536]{2,1,0:T(8,128)(2,1)}, u32[]{:S(2)}, u32[]{:S(2)}) collective-permute-start(bf16[4,48,1536]{2,1,0:T(8,128)(2,1)S(1)} %get-tuple-element.218), channel_id=1, source_target_pairs={{0,2},{1,5},{2,0},{3,7},{4,6},{5,1},{6,4},{7,3},{8,10},{9,13},{10,... | collective-permute-start | bytes 1769480 | tf_op jit(solution)/shard_map/ppermute | solution.py:678
  193.7 23.4 %collective-permute-start.28 = (bf16[8,48,1536]{2,1,0:T(8,128)(2,1)}, bf16[8,48,1536]{2,1,0:T(8,128)(2,1)}, u32[]{:S(2)}, u32[]{:S(2)}) collective-permute-start(bf16[8,48,1536]{2,1,0:T(8,128)(2,1)} %get-tuple-element.171), channel_id=1, source_target_pairs={{0,4},{1,3},{2,6},{3,1},{4,0},{5,7},{6,2},{7,5},{8,12},{9,11},{10,... | collective-permute-start | bytes 3538952 | tf_op jit(solution)/shard_map/ppermute | solution.py:678
  212.4 18.4 %collective-permute-start.27 = (bf16[2,128,768]{2,1,0:T(8,128)(2,1)}, bf16[2,128,768]{2,1,0:T(8,128)(2,1)}, u32[]{:S(2)}, u32[]{:S(2)}) collective-permute-start(bf16[2,128,768]{2,1,0:T(8,128)(2,1)} %get-tuple-element.170), channel_id=1, source_target_pairs={{0,3},{1,2},{2,1},{3,0},{4,7},{5,6},{6,5},{7,4},{8,11},{9,10},{10,... | collective-permute-start | bytes 1179656 | tf_op jit(solution)/shard_map/ppermute | solution.py:764
  213.3 20.7 %collective-permute-start.31 = (bf16[2,96,768]{2,1,0:T(8,128)(2,1)S(1)}, bf16[2,96,768]{2,1,0:T(8,128)(2,1)S(1)}, u32[]{:S(2)}, u32[]{:S(2)}) collective-permute-start(bf16[2,96,768]{2,1,0:T(8,128)(2,1)S(1)} %add_convert_fusion.12), channel_id=1, source_target_pairs={{0,8},{1,9},{2,10},{3,11},{4,12},{5,13},{6,14},{7,15},{8,0},{9,1},... | collective-permute-start | bytes 884744 | tf_op jit(solution)/shard_map/ppermute | solution.py:678
  217.2 18.4 %collective-permute-start.30 = (bf16[2,48,1536]{2,1,0:T(8,128)(2,1)S(1)}, bf16[2,48,1536]{2,1,0:T(8,128)(2,1)}, u32[]{:S(2)}, u32[]{:S(2)}) collective-permute-start(bf16[2,48,1536]{2,1,0:T(8,128)(2,1)S(1)} %add_convert_fusion.11), channel_id=1, source_target_pairs={{0,16},{1,17},{2,18},{3,19},{4,20},{5,21},{6,22},{7,23},{8,24},{9,... | collective-permute-start | bytes 884744 | tf_op jit(solution)/shard_map/ppermute | solution.py:678
  247.3 25.4 %collective-permute-start.40 = (bf16[8,96,768]{2,1,0:T(8,128)(2,1)S(1)}, bf16[8,96,768]{2,1,0:T(8,128)(2,1)S(1)}, u32[]{:S(2)}, u32[]{:S(2)}) collective-permute-start(bf16[8,96,768]{2,1,0:T(8,128)(2,1)S(1)} %pad_maximum_fusion.3), channel_id=1, source_target_pairs={{0,4},{1,3},{2,6},{3,1},{4,0},{5,7},{6,2},{7,5},{8,12},{9,11},{10,... | collective-permute-start | bytes 3538952 | tf_op jit(solution)/shard_map/ppermute | solution.py:678
  272.9 20.1 %collective-permute-start.44 = (bf16[16,96,768]{2,1,0:T(8,128)(2,1)S(1)}, bf16[16,96,768]{2,1,0:T(8,128)(2,1)}, u32[]{:S(2)}, u32[]{:S(2)}) collective-permute-start(bf16[16,96,768]{2,1,0:T(8,128)(2,1)S(1)} %pad_maximum_fusion.half_ref), channel_id=1, source_target_pairs={{0,1},{1,0},{2,3},{3,2},{4,5},{5,4},{6,7},{7,6},{8,9},{9,8},{10,11... | collective-permute-start | bytes 7077896 | tf_op jit(solution)/shard_map/ppermute | solution.py:678
  273.4 19.7 %collective-permute-start.43 = (bf16[8,48,1536]{2,1,0:T(8,128)(2,1)}, bf16[8,48,1536]{2,1,0:T(8,128)(2,1)}, u32[]{:S(2)}, u32[]{:S(2)}) collective-permute-start(bf16[8,48,1536]{2,1,0:T(8,128)(2,1)} %pad_maximum_fusion.4), channel_id=1, source_target_pairs={{0,4},{1,3},{2,6},{3,1},{4,0},{5,7},{6,2},{7,5},{8,12},{9,11},{10,... | collective-permute-start | bytes 3538952 | tf_op jit(solution)/shard_map/ppermute | solution.py:678
  294.8 21.1 %collective-permute-start.47 = (bf16[16,48,1536]{2,1,0:T(8,128)(2,1)S(1)}, bf16[16,48,1536]{2,1,0:T(8,128)(2,1)}, u32[]{:S(2)}, u32[]{:S(2)}) collective-permute-start(bf16[16,48,1536]{2,1,0:T(8,128)(2,1)S(1)} %pad_maximum_fusion.1.half_ref), channel_id=1, source_target_pairs={{0,1},{1,0},{2,3},{3,2},{4,5},{5,4},{6,7},{7,6},{8,9},{9,8},{10,11... | collective-permute-start | bytes 7077896 | tf_op jit(solution)/shard_map/ppermute | solution.py:678
  306.0 18.5 %collective-permute-start.46 = (bf16[8,48,1536]{2,1,0:T(8,128)(2,1)}, bf16[8,48,1536]{2,1,0:T(8,128)(2,1)}, u32[]{:S(2)}, u32[]{:S(2)}) collective-permute-start(bf16[8,48,1536]{2,1,0:T(8,128)(2,1)} %pad_maximum_fusion.5), channel_id=1, source_target_pairs={{0,4},{1,3},{2,6},{3,1},{4,0},{5,7},{6,2},{7,5},{8,12},{9,11},{10,... | collective-permute-start | bytes 3538952 | tf_op jit(solution)/shard_map/ppermute | solution.py:678
  (60 other events, 515.5 us)
